TPU v7x, 32 devices: a whole 2x2x4 slice. The times are simulated.
32 devices in a mesh: ctx: 8 (over z, x), exp: 4 (over y, core).
Axes of the slice: x: 2, y: 2, z: 4, core: 2. Of those that a mesh axis runs over, the one named last changes fastest.
Arguments:
- queries: bfloat16 [512, 6144], P('exp', 'ctx'), may hold values from -4 to 4
- key_vectors: bfloat16 [512, 6144], P('exp', 'ctx'), may hold values from -4 to 4
- value_vectors: bfloat16 [512, 6144], P('exp', 'ctx'), may hold values from -6 to 6
- decay_slopes: float32 [64], P('ctx'), may hold values from 0.0001 to 0.1
- residual: bfloat16 [512, 6144], P(('exp', 'ctx')), may hold values from -6 to 6
- mixer_gain: float32 [6144], replicated, may hold values from 0.25 to 1.75
- expert_gain: float32 [6144], replicated, may hold values from 0.25 to 1.75
- up_weight: bfloat16 [4, 9216, 6144], P('exp', 'ctx'), may hold values from -0.078125 to 0.078125
- down_weight: bfloat16 [4, 9216, 6144], P('exp', 'ctx'), may hold values from -0.0625 to 0.0625
- expert_ids: int32 [512, 2], P('exp'), may hold values from 0 to 3, all different within a row; in each aligned block of 128 rows (0 to 127, 128 to 255, ...) at most 68 rows name the same one
- gate_code: int32 [512, 2], P('exp'), may hold values from 0 to 15
- cotangent: bfloat16 [512, 6144], P(('exp', 'ctx')), may hold values from -6 to 6
Outputs:
- layer_output: bfloat16 [512, 6144], P(('exp', 'ctx'))
- residual_grad: bfloat16 [512, 6144], P(('exp', 'ctx'))
- query_grad: bfloat16 [512, 6144], P('exp', 'ctx')
- key_grad: bfloat16 [512, 6144], P('exp', 'ctx')
- value_grad: bfloat16 [512, 6144], P('exp', 'ctx')
Inputs may be any that keep to these rules, and one draw needn't show every extreme that they name: `expert_ids`: each row names two different experts; in each aligned block of 128 rows (one sequence block) no expert is named by more than 68 rows.
All inputs are finite; a program needn't handle non-finite values.
Results may differ from a plain program's by a relative error of at most 0.0095.
Values may be sent and summed in bfloat16 or wider, within the bound.
No kernel may reach another device: no remote copies, remote signals or barrier semaphores. Data moves between devices by JAX's collectives and lax.ppermute only.
A program may use at most 256 MiB of HBM per device.

v0:
```python
import jax
import jax.numpy as jnp
from jax import lax
from jax.experimental import pallas as pl
from jax.experimental.pallas import tpu as pltpu
from jax.sharding import PartitionSpec as P

EPSILON = 1e-06
HIGHEST = lax.Precision.HIGHEST
BF16 = jnp.bfloat16
F32 = jnp.float32


def span_output(query_rows, key_rows, value_rows, entering, slope):
    length = query_rows.shape[0]
    places = jnp.arange(length).astype(jnp.float32)
    spacing = places[:, None] - places[None, :]
    fading = jnp.where(spacing >= 0.0, jnp.exp(-slope * jnp.maximum(spacing, 0.0)), 0.0)
    scores = jnp.dot(query_rows, key_rows.T, preferred_element_type=jnp.float32)
    weights = (scores * fading).astype(jnp.bfloat16)
    inner = jnp.dot(weights, value_rows, preferred_element_type=jnp.float32)
    carried = jnp.dot(query_rows.astype(jnp.float32), entering, precision=HIGHEST)
    return inner + carried * jnp.exp(-slope * (places + 1.0))[:, None]


def span_summary(key_rows, value_rows, slope):
    length = key_rows.shape[0]
    places = jnp.arange(length).astype(jnp.float32)
    faded = key_rows.astype(jnp.float32) * jnp.exp(-slope * (length - 1.0 - places))[:, None]
    return jnp.dot(faded.T, value_rows.astype(jnp.float32), precision=HIGHEST)


def span_pair(query_rows, key_rows, value_rows, entering, slope):
    return (
        span_output(query_rows, key_rows, value_rows, entering, slope),
        span_summary(key_rows, value_rows, slope),
    )


def state_grad(query_rows, grad_rows, slope):
    length = query_rows.shape[0]
    places = jnp.arange(length).astype(jnp.float32)
    faded = query_rows.astype(jnp.float32) * jnp.exp(-slope * (places + 1.0))[:, None]
    return jnp.dot(faded.T, grad_rows.astype(jnp.float32), precision=HIGHEST)


def span_backward(query_rows, key_rows, value_rows, entering, slope, grad_rows, grad_state):

    def local_pair(first, second, third):
        return span_pair(first, second, third, entering, slope)

    _, pullback = jax.vjp(local_pair, query_rows, key_rows, value_rows)
    return pullback((grad_rows.astype(jnp.float32), grad_state))


def silu_slope(before):
    sigma = jax.nn.sigmoid(before)
    return sigma * (1.0 + before * (1.0 - sigma))


def ring_order(size):
    if size == 8:
        return [0, 2, 4, 6, 7, 5, 3, 1]
    return list(range(size))


class Ring:
    def __init__(self):
        self.size = lax.axis_size("ctx")
        order = ring_order(self.size)
        self.right = [(order[i], order[(i + 1) % self.size]) for i in range(self.size)]
        self.left = [(b, a) for a, b in self.right]
        place = [order.index(i) for i in range(self.size)]
        self.order = jnp.array(order, jnp.int32)
        self.place = jnp.array(place, jnp.int32)[lax.axis_index("ctx")]

    def at(self, offset):
        return self.order[(self.place + offset) % self.size]

    def go_right(self, x):
        return lax.ppermute(x, "ctx", self.right)

    def go_left(self, x):
        return lax.ppermute(x, "ctx", self.left)


def swap(x, k):
    return lax.ppermute(x, "exp", [(i, i ^ k) for i in range(lax.axis_size("exp"))])


def ctx_sum(x):
    size = lax.axis_size("ctx")
    step = 1
    while step < size:
        x = x + lax.ppermute(x, "ctx", [(i, i ^ step) for i in range(size)])
        step *= 2
    return x


def ring_sum(partial, ring):
    far = partial[4]
    rows = far.shape[0]
    low = far.astype(BF16)
    to_right, to_left = low[: rows // 2], low[rows // 2 :]
    blank = jnp.zeros_like(to_right)
    to_right = jnp.concatenate([ring.go_right(to_right), blank], axis=0)
    to_left = jnp.concatenate([blank, ring.go_left(to_left)], axis=0)
    for offset in (3, 2, 1):
        to_right = ring.go_right((partial[offset] + to_right.astype(F32)).astype(BF16))
        to_left = ring.go_left((partial[-offset] + to_left.astype(F32)).astype(BF16))
    return partial[0] + to_right.astype(F32) + to_left.astype(F32)


def ring_block(size, offset):
    here = lax.axis_index("ctx")
    row, column = here // 2, here % 2
    place = row + column * (size - 1 - 2 * row)
    at = (place + offset + size) % size
    far = at // (size // 2)
    return 2 * at + far * (2 * size - 1 - 4 * at)


def columns(weight_ref, block, size):
    width = weight_ref.shape[1] // size
    return weight_ref[:, pl.ds(pl.multiple_of(block * width, width), width)]


WHOLE = pl.BlockSpec(memory_space=pltpu.VMEM)
ANYWHERE = pl.BlockSpec(memory_space=pl.ANY)
IN_HBM = pl.BlockSpec(memory_space=pltpu.HBM)
NT = (((1,), (1,)), ((), ()))


def cost(rows, hidden, width):
    return pl.CostEstimate(
        flops=2 * rows * hidden * width, bytes_accessed=2 * hidden * width, transcendentals=0
    )


def load_call(arrays, after=()):
    count = len(arrays)

    def kernel(*refs):
        sources, targets, arrived = refs[:count], refs[-1 - count : -1], refs[-1]
        copies = [
            pltpu.make_async_copy(source, target, arrived.at[k])
            for k, (source, target) in enumerate(zip(sources, targets))
        ]
        for copy in copies:
            copy.start()
        for copy in copies:
            copy.wait()

    return pl.pallas_call(
        kernel,
        in_specs=[IN_HBM] * count + [ANYWHERE] * len(after),
        out_specs=[WHOLE] * count,
        out_shape=[pltpu.VMEM(x.shape, x.dtype) for x in arrays],
        scratch_shapes=[pltpu.SemaphoreType.DMA((count,))],
        compiler_params=pltpu.CompilerParams(vmem_limit_bytes=32 * 2**20),
        name="load_weights",
    )(*arrays, *after)


def backward_call(rows_all, weight, before, share, after=()):
    rows, features = rows_all.shape
    hidden = weight.shape[0]
    span, parts = rows // 4, 4
    part = features // parts

    def kernel(rows_ref, weight_ref, before_ref, share_ref, *refs):
        out_ref, held, total, landed = refs[-4:]
        mine = lax.axis_index("exp")
        core, side = lax.rem(mine, 2), mine // 2

        def fetch(k):
            copies = []
            for j, (flip_side, flip_core) in enumerate(((0, 0), (1, 0), (0, 1), (1, 1))):
                block = 2 * (side + flip_side * (1 - 2 * side)) + core
                block = block + flip_core * (1 - 2 * core)
                copies.append(
                    pltpu.make_async_copy(
                        rows_ref.at[
                            pl.ds(pl.multiple_of(block * span, span), span),
                            pl.ds(k * part, part),
                        ],
                        held.at[k % 2, pl.ds(j * span, span), :],
                        landed.at[k % 2, j],
                    )
                )
                copies[-1].start()
            return copies

        coming = fetch(0)
        for k in range(parts):
            arrived = coming
            if k + 1 < parts:
                coming = fetch(k + 1)
            for copy in arrived:
                copy.wait()
            value = lax.dot_general(
                held[k % 2],
                weight_ref[:, pl.ds(k * part, part)],
                NT,
                preferred_element_type=F32,
            )
            total[...] = value if k == 0 else total[...] + value
        here, share = before_ref[...], share_ref[...]
        sigma = 1.0 / (1.0 + jnp.exp(-here))
        value = share * total[...] * (sigma * (1.0 + here * (1.0 - sigma)))
        out_ref[...] = jnp.where(share > 0.0, value, 0.0).astype(BF16)

    return pl.pallas_call(
        kernel,
        in_specs=[IN_HBM] + [WHOLE] * 3 + [ANYWHERE] * len(after),
        out_specs=WHOLE,
        out_shape=jax.ShapeDtypeStruct((rows, hidden), BF16),
        scratch_shapes=[
            pltpu.VMEM((2, rows, part), BF16),
            pltpu.VMEM((rows, hidden), F32),
            pltpu.SemaphoreType.DMA((2, 4)),
        ],
        compiler_params=pltpu.CompilerParams(vmem_limit_bytes=10 * 2**20),
        cost_estimate=cost(rows, hidden, features),
        name="backward_rows",
    )(rows_all, weight, before, share, *after)


def before_call(found, ring, offsets, weight, gain, start=None, share=None, after=()):
    count = len(offsets)
    pieces = [part for o in offsets for part in found[o]]
    half, width = pieces[0].shape
    rows, hidden, features, size = 2 * half, weight.shape[0], weight.shape[1], ring.size
    gain = gain.reshape(size, width)
    sums = [jax.ShapeDtypeStruct((rows, hidden), F32), jax.ShapeDtypeStruct((rows, 1), F32)]
    first, last = start is None, share is not None

    def kernel(weight_ref, gain_ref, *refs):
        refs = list(refs)
        parts = [refs.pop(0) for _ in pieces]
        begin = [] if first else [refs.pop(0), refs.pop(0)]
        share_ref = refs.pop(0) if last else None
        refs = refs[len(after) :]
        total, other = refs.pop(0), refs.pop(0)
        held, scaled, landed = refs[:3]
        copies = []
        for k in range(count):
            for side in range(2):
                copies.append(
                    pltpu.make_async_copy(
                        parts[2 * k + side],
                        held.at[k, pl.ds(side * half, half), :],
                        landed.at[2 * k + side],
                    )
                )
                copies[-1].start()
        square = None if first else begin[1][...]
        for k in range(count):
            copies[2 * k].wait()
            copies[2 * k + 1].wait()
            value = held[k].astype(F32)
            squares = jnp.sum(value * value, axis=-1, keepdims=True)
            square = squares if square is None else square + squares
            block = ring_block(size, offsets[k])
            scaled[...] = (value * gain_ref[pl.ds(block, 1), :]).astype(BF16)
            product = lax.dot_general(
                scaled[...], columns(weight_ref, block, size), NT, preferred_element_type=F32
            )
            if k == 0:
                total[...] = product if first else begin[0][...] + product
            else:
                total[...] += product
        if last:
            before = total[...] * lax.rsqrt(square / features + EPSILON)
            total[...] = before
            active = before * (1.0 / (1.0 + jnp.exp(-before)))
            other[...] = jnp.where(share_ref[...] > 0.0, active, 0.0).astype(BF16)
        else:
            other[...] = square

    rest = list(start or ()) + ([share] if last else [])
    return pl.pallas_call(
        kernel,
        in_specs=[WHOLE, WHOLE]
        + [ANYWHERE] * len(pieces)
        + [WHOLE] * len(rest)
        + [ANYWHERE] * len(after),
        out_specs=[WHOLE, WHOLE],
        out_shape=[sums[0], jax.ShapeDtypeStruct((rows, hidden), BF16) if last else sums[1]],
        scratch_shapes=[
            pltpu.VMEM((count, rows, width), BF16),
            pltpu.VMEM((rows, width), BF16),
            pltpu.SemaphoreType.DMA((2 * count,)),
        ],
        compiler_params=pltpu.CompilerParams(vmem_limit_bytes=8 * 2**20),
        cost_estimate=cost(rows, hidden, count * width),
        name="before_rows",
    )(weight, gain, *pieces, *rest, *after)


def second_call(left, ring, offsets, weight, share=None, after=()):
    count = len(offsets)
    rows, hidden = left.shape
    half, size = rows // 2, ring.size
    width = weight.shape[1] // size

    def kernel(weight_ref, left_ref, *refs):
        keep_ref, give_ref = refs[-2:]
        for k in range(count):
            block = ring_block(size, offsets[k])
            value = jnp.dot(
                left_ref[...], columns(weight_ref, block, size), preferred_element_type=F32
            )
            if share is not None:
                value = value * refs[0][...]
            keep_ref[k] = value[:half].astype(BF16)
            give_ref[k] = value[half:].astype(BF16)

    extra = [] if share is None else [share]
    return pl.pallas_call(
        kernel,
        in_specs=[WHOLE] * (2 + len(extra)) + [ANYWHERE] * len(after),
        out_specs=[WHOLE, WHOLE],
        out_shape=[jax.ShapeDtypeStruct((count, half, width), BF16)] * 2,
        compiler_params=pltpu.CompilerParams(vmem_limit_bytes=8 * 2**20),
        cost_estimate=cost(rows, hidden, count * width),
        name="partial_rows",
    )(weight, left, *extra, *after)


def turn_call(residual, cotangent, after, ring):
    rows, features = residual.shape
    width = features // ring.size

    def kernel(residual_ref, cotangent_ref, after_ref, out_ref):
        for k in range(ring.size):
            span = pl.ds(k * width, width)
            out_ref[k, pl.ds(0, rows), :] = residual_ref[:, span]
            out_ref[k, pl.ds(rows, rows), :] = cotangent_ref[:, span]

    return pl.pallas_call(
        kernel,
        in_specs=[WHOLE, WHOLE, ANYWHERE],
        out_specs=WHOLE,
        out_shape=jax.ShapeDtypeStruct((ring.size, 2 * rows, width), BF16),
        name="turn",
    )(residual, cotangent, after)


def fast_device(
    queries,
    key_vectors,
    value_vectors,
    decay_slopes,
    residual,
    mixer_gain,
    expert_gain,
    up_weight,
    down_weight,
    expert_ids,
    gate_code,
    cotangent,
):
    length, width = queries.shape
    features = residual.shape[1]
    local_heads = decay_slopes.shape[0]
    head_width = width // local_heads
    ring = Ring()
    here, mine = lax.axis_index("ctx"), lax.axis_index("exp")
    core = mine % 2

    cot_all = lax.all_gather(cotangent, ("exp", "ctx"), axis=0, tiled=True)

    codes = (expert_ids * 16 + gate_code).astype(F32)
    codes = jnp.concatenate([codes, swap(codes, 2)], axis=0)
    codes = jnp.concatenate([codes, swap(codes, 1)], axis=0).astype(jnp.int32)
    share = jnp.where(codes // 16 == mine, (1.0 + (codes % 16).astype(F32)) / 16.0, 0.0)
    share = jnp.sum(share, axis=-1, keepdims=True)

    query_heads = queries.reshape(length, local_heads, head_width)
    key_heads = key_vectors.reshape(length, local_heads, head_width)
    value_heads = value_vectors.reshape(length, local_heads, head_width)
    fade = jnp.exp(-decay_slopes * length)[:, None, None]
    summary = jax.vmap(span_summary, in_axes=(1, 1, 0))(key_heads, value_heads, decay_slopes)
    other = swap(summary, 1)
    pair = jnp.where(core == 0, fade * summary + other, fade * other + summary)
    both = turn_call(residual, cotangent, other, ring)
    both = lax.all_to_all(both, "ctx", split_axis=0, concat_axis=0, tiled=True)
    both = both.reshape(ring.size, 2, -1, width)
    residual_part = both[:, 0].reshape(length, width)
    cot_part = both[:, 1].reshape(length, width)
    before_pair = lax.ppermute(pair, "exp", [(0, 2), (1, 3)])
    entering = jnp.where(core == 0, before_pair, fade * before_pair + other)
    mixed_heads = jax.vmap(span_output, in_axes=(1, 1, 1, 0, 0), out_axes=1)(
        query_heads, key_heads, value_heads, entering, decay_slopes
    )
    mixed_low = lax.optimization_barrier(mixed_heads.reshape(length, width).astype(BF16))
    mixed = mixed_low.astype(F32)
    mix_gain = lax.dynamic_slice(mixer_gain, (here * width,), (width,))
    exp_gain = lax.dynamic_slice(expert_gain, (here * width,), (width,))
    mixed_square = ctx_sum(jnp.sum(mixed * mixed, axis=-1)[None])[0][:, None]
    scale_1 = lax.rsqrt(mixed_square / features + EPSILON)
    hidden_low = (residual_part.astype(F32) + mixed * scale_1 * mix_gain).astype(BF16)
    hidden_low = lax.optimization_barrier(hidden_low)
    hidden = hidden_low.astype(F32)
    across = swap(hidden_low, 2)
    rights, lefts = [hidden_low], [hidden_low]
    for step in range(1, 5):
        rights.append(ring.go_right(rights[-1]))
        if step < 4:
            lefts.append(ring.go_left(lefts[-1]))
    cot = cot_part.astype(F32)
    early = jnp.stack(
        [
            jnp.sum(hidden * hidden, axis=-1),
            jnp.sum(mix_gain * mixed * cot, axis=-1),
            jnp.sum(mix_gain * mixed * hidden, axis=-1),
        ]
    )

    up_hidden, down_hidden = load_call((up_weight[0], down_weight[0]), (across,))
    found = {}
    for step in range(5):
        for offset, rows in ((-step, rights), (step, lefts)):
            if (step < 4 and (step > 0 or rows is rights)) or (step == 4 and rows is rights):
                own = rows[step]
                own = jnp.concatenate([own, across if step == 0 else swap(own, 2)], axis=0)
                found[4 if step == 4 else offset] = (own, swap(own, 1))

    def before_part(offsets, sums=None, share=None, after=()):
        return before_call(found, ring, offsets, up_hidden, expert_gain, sums, share, after)

    sums = before_part((0,), after=(rights[3],))
    sums = before_part((-1, 1), sums, after=(rights[4],))
    sums = before_part((-2, 2), sums)
    sums = before_part((-3, 3), sums)
    before, active = before_part((4,), sums, share)

    in_parts, out_parts = {}, {}

    def second(left, offsets, weight, parts, scale, after):
        keep, give = second_call(left, ring, offsets, weight, scale, after)
        got = swap(give, 1)
        for i, offset in enumerate(offsets):
            parts[offset] = keep[i].astype(F32) + got[i].astype(F32)
        return give, got

    def second_in(offsets, *after):
        return second(inner_grad, offsets, up_hidden, in_parts, None, after)

    def second_out(offsets, *after):
        return second(active, offsets, down_hidden, out_parts, share, after)

    def cross(offsets):
        far = jnp.stack([in_parts[o][length:].astype(BF16) for o in offsets])
        far = swap(far, 2)
        for i, o in enumerate(offsets):
            in_parts[o] = in_parts[o][:length] + far[i].astype(F32)
        return far

    give, got_a = second_out((4,))
    give, got_b = second_out((3, -3), give)
    inner_grad = backward_call(cot_all, down_hidden, before, share, (give, got_a))
    give, got_c = second_in((4,))
    far_0 = cross((4,))
    give, got_d = second_in((3, -3), give, got_b)
    far_1 = cross((3, -3))
    give, got_e = second_out((2, -2), give, got_c)
    give, got_f = second_in((2, -2), give, got_d)
    cross((2, -2))
    give, _ = second_out((1, -1), give, got_e, far_0)
    give, got_g = second_in((1, -1), give, got_f)
    cross((1, -1))
    give, _ = second_out((0,), give, far_1)
    second_in((0,), give, got_g)
    cross((0,))
    collected = ring_sum(in_parts, ring)
    combined = ring_sum(out_parts, ring)
    combined = combined[:length] + swap(combined[length:].astype(BF16), 2).astype(F32)

    gained = exp_gain * collected
    late = jnp.stack(
        [jnp.sum(gained * hidden, axis=-1), jnp.sum(mix_gain * mixed * gained, axis=-1)]
    )
    hidden_square, along_cot, along_hidden, along_gained, along_mixed = ctx_sum(
        jnp.concatenate([early, late], axis=0)
    )[:, :, None]
    scale_2 = lax.rsqrt(hidden_square / features + EPSILON)
    pull_2 = scale_2 * scale_2 * scale_2 / features * along_gained
    hidden_grad = cot + scale_2 * gained - hidden * pull_2
    along = along_cot + scale_2 * along_mixed - pull_2 * along_hidden
    mixed_grad = scale_1 * (mix_gain * hidden_grad) - mixed * (
        scale_1 * scale_1 * scale_1 / features * along
    )
    grad_heads = lax.optimization_barrier(mixed_grad.astype(BF16))
    grad_heads = grad_heads.reshape(length, local_heads, head_width)
    ends = jnp.concatenate(
        [x.astype(BF16).reshape(ring.size, -1, width) for x in (hidden_grad, hidden + combined)],
        axis=1,
    )
    ends = lax.all_to_all(ends, "ctx", split_axis=0, concat_axis=0, tiled=True)
    ends = ends.transpose(1, 0, 2).reshape(2, -1, features)
    residual_grad, layer_output = ends[0], ends[1]

    block_grad = jax.vmap(state_grad, in_axes=(1, 1, 0))(query_heads, grad_heads, decay_slopes)
    other = swap(block_grad, 1)
    pair = jnp.where(core == 0, block_grad + fade * other, other + fade * block_grad)
    after_pair = lax.ppermute(pair, "exp", [(2, 0), (3, 1)])
    later = jnp.where(core == 0, other + fade * after_pair, after_pair)
    query_grad, key_grad, value_grad = jax.vmap(
        span_backward, in_axes=(1, 1, 1, 0, 0, 1, 0), out_axes=1
    )(query_heads, key_heads, value_heads, entering, decay_slopes, grad_heads, later)
    return (
        layer_output,
        residual_grad,
        query_grad.reshape(length, -1),
        key_grad.reshape(length, -1),
        value_grad.reshape(length, -1),
    )


def entering_2(x, axis, combine, identity, reverse):
    count, position = (lax.axis_size(axis), lax.axis_index(axis))
    everything = jax.tree.map(lambda part: lax.all_gather(part, axis), x)
    start = jax.tree.map(
        lambda part, zero: jnp.broadcast_to(jnp.asarray(zero, part.dtype), part.shape), x, identity
    )

    def lap(k, before):
        at = count - 1 - k if reverse else k
        reached = at > position if reverse else at < position
        new = combine(before, jax.tree.map(lambda part: part[at], everything))
        return jax.tree.map(lambda a, b: jnp.where(reached, a, b), new, before)

    return lax.fori_loop(0, count, lap, start)


def rms_gain(values, gain):
    return values * lax.rsqrt(jnp.mean(values * values, axis=-1, keepdims=True) + EPSILON) * gain


def chain(earlier, later):
    return (earlier[0] * later[0], later[0][:, None, None] * earlier[1] + later[1])


def per_device(
    queries,
    key_vectors,
    value_vectors,
    decay_slopes,
    residual,
    mixer_gain,
    expert_gain,
    up_weight,
    down_weight,
    expert_ids,
    gate_code,
    cotangent,
):
    length = queries.shape[0]
    local_heads = decay_slopes.shape[0]
    head_width = queries.shape[1] // local_heads
    query_heads = queries.reshape(length, local_heads, head_width)
    key_heads = key_vectors.reshape(length, local_heads, head_width)
    value_heads = value_vectors.reshape(length, local_heads, head_width)
    block_fade = jnp.exp(-decay_slopes * length)
    summary = jax.vmap(span_summary, in_axes=(1, 1, 0))(key_heads, value_heads, decay_slopes)
    identity = (jnp.ones_like(block_fade), jnp.zeros_like(summary))
    entering = entering_2((block_fade, summary), "exp", chain, identity, False)[1]
    mixed_heads = jax.vmap(span_output, in_axes=(1, 1, 1, 0, 0), out_axes=1)(
        query_heads, key_heads, value_heads, entering, decay_slopes
    )
    mixed_heads = mixed_heads.astype(jnp.bfloat16).reshape(length, -1)
    mixed_low = lax.all_to_all(mixed_heads, "ctx", split_axis=0, concat_axis=1, tiled=True)
    mixed = mixed_low.astype(jnp.float32)
    hidden_low = (residual.astype(jnp.float32) + rms_gain(mixed, mixer_gain)).astype(jnp.bfloat16)
    hidden = lax.optimization_barrier(hidden_low).astype(jnp.float32)
    normed = rms_gain(hidden, expert_gain).astype(jnp.bfloat16)
    groups = lax.axis_size("exp")
    block_len = expert_ids.shape[0]
    capacity = min(block_len, max(2, 17 * block_len // (8 * groups)))
    share = ((1.0 + gate_code.astype(jnp.float32)) / 16.0).reshape(-1)
    flat = expert_ids.reshape(-1)
    marks = (flat[:, None] == jnp.arange(groups, dtype=jnp.int32)[None, :]).astype(jnp.int32)
    slots = jnp.sum((jnp.cumsum(marks, axis=0) - marks) * marks, axis=1)
    target = flat * capacity + slots
    matching = target[None, :] == jnp.arange(groups * capacity, dtype=jnp.int32)[:, None]
    filled = jnp.any(matching, axis=1)
    source_route = jnp.sum(
        jnp.where(matching, jnp.arange(2 * block_len, dtype=jnp.int32)[None, :], 0), axis=1
    )
    source_token = source_route // 2
    slot_share = jnp.take(share, source_route)
    up_hidden = up_weight[0]
    down_hidden = down_weight[0]
    block_normed, block_cot = (
        lax.all_gather(normed, "ctx", axis=0, tiled=True),
        lax.all_gather(cotangent, "ctx", axis=0, tiled=True),
    )
    taken = jnp.take(block_normed, source_token, axis=0)
    rows = jnp.where(filled[:, None], taken, jnp.zeros_like(taken))
    weighted = jnp.take(block_cot, source_token, axis=0).astype(jnp.float32) * slot_share[:, None]
    grads = jnp.where(filled[:, None], weighted, 0.0).astype(jnp.bfloat16)
    send_rows = rows.reshape(groups, capacity, -1)
    send_grad = grads.reshape(groups, capacity, -1)
    pieces = (
        lax.all_to_all(send_rows, "exp", split_axis=0, concat_axis=0, tiled=True),
        lax.all_to_all(send_grad, "exp", split_axis=0, concat_axis=0, tiled=True),
    )
    before = jnp.einsum("bsd,hd->bsh", pieces[0], up_hidden, preferred_element_type=jnp.float32)
    backward = jnp.einsum("bsd,hd->bsh", pieces[1], down_hidden, preferred_element_type=jnp.float32)
    before = before.reshape(-1, before.shape[-1])
    backward = backward.reshape(-1, backward.shape[-1])
    active = jax.nn.silu(before).astype(jnp.bfloat16)
    inner_grad = (backward * silu_slope(before)).astype(jnp.bfloat16)
    up_moved, down_moved = (
        lax.all_to_all(up_weight, "ctx", split_axis=2, concat_axis=1, tiled=True),
        lax.all_to_all(down_weight, "ctx", split_axis=2, concat_axis=1, tiled=True),
    )
    up_features = up_moved[0]
    down_features = down_moved[0]
    pieces = (
        lax.all_gather(active, "ctx", axis=1, tiled=True),
        lax.all_gather(inner_grad, "ctx", axis=1, tiled=True),
    )
    out_total = jnp.dot(pieces[0], down_features, preferred_element_type=jnp.float32)
    in_total = jnp.dot(pieces[1], up_features, preferred_element_type=jnp.float32)
    columns = down_features.shape[1]
    result = out_total.astype(jnp.bfloat16).reshape(groups, capacity, columns)
    input_grad = in_total.astype(jnp.bfloat16).reshape(groups, capacity, columns)
    back_rows, back_grad = (
        lax.all_to_all(result, "exp", split_axis=0, concat_axis=0, tiled=True),
        lax.all_to_all(input_grad, "exp", split_axis=0, concat_axis=0, tiled=True),
    )
    back_rows = back_rows.reshape(groups * capacity, columns)
    back_grad = back_grad.reshape(groups * capacity, columns)
    route_result = jnp.take(back_rows, target, axis=0).astype(jnp.float32)
    route_grad = jnp.take(back_grad, target, axis=0).astype(jnp.float32)
    combined = jnp.sum((route_result * share[:, None]).reshape(block_len, 2, columns), axis=1)
    collected = jnp.sum(route_grad.reshape(block_len, 2, columns), axis=1)
    combined_rows, collected_rows = (
        lax.all_to_all(combined, "ctx", split_axis=0, concat_axis=1, tiled=True),
        lax.all_to_all(collected, "ctx", split_axis=0, concat_axis=1, tiled=True),
    )
    layer_output = (hidden + combined_rows).astype(jnp.bfloat16)
    _, pull_expert = jax.vjp(lambda values: rms_gain(values, expert_gain), hidden)
    hidden_grad = cotangent.astype(jnp.float32) + pull_expert(collected_rows)[0]
    residual_grad = hidden_grad.astype(jnp.bfloat16)
    _, pull_mixer = jax.vjp(lambda values: rms_gain(values, mixer_gain), mixed)
    mixed_grad = pull_mixer(hidden_grad)[0].astype(jnp.bfloat16)
    grad_heads = lax.all_to_all(mixed_grad, "ctx", split_axis=1, concat_axis=0, tiled=True).reshape(
        length, local_heads, head_width
    )
    block_grad = jax.vmap(state_grad, in_axes=(1, 1, 0))(query_heads, grad_heads, decay_slopes)
    later = entering_2((block_fade, block_grad), "exp", chain, identity, True)[1]
    query_grad, key_grad, value_grad = jax.vmap(
        span_backward, in_axes=(1, 1, 1, 0, 0, 1, 0), out_axes=1
    )(query_heads, key_heads, value_heads, entering, decay_slopes, grad_heads, later)
    return (
        layer_output,
        residual_grad,
        query_grad.reshape(length, -1),
        key_grad.reshape(length, -1),
        value_grad.reshape(length, -1),
    )


def solution(mesh):
    in_specs = (
        P("exp", "ctx"),
        P("exp", "ctx"),
        P("exp", "ctx"),
        P("ctx"),
        P(("exp", "ctx"), None),
        P(),
        P(),
        P("exp", "ctx", None),
        P("exp", "ctx", None),
        P("exp", None),
        P("exp", None),
        P(("exp", "ctx"), None),
    )
    out_specs = (
        P(("exp", "ctx"), None),
        P(("exp", "ctx"), None),
        P("exp", "ctx"),
        P("exp", "ctx"),
        P("exp", "ctx"),
    )
    fast = mesh.shape["ctx"] == 8 and mesh.shape["exp"] == 4
    body = fast_device if fast else per_device
    return jax.shard_map(
        body, mesh=mesh, in_specs=in_specs, out_specs=out_specs, check_vma=False
    )
```

profile of v0, /device:TPU:0, one launch (start us, length us, event | category | flops | bytes accessed | tf_op | source)
XLA Modules:
  0.0 283.4 jit_solution(733676718796975051)
XLA Ops:
  13.8 4.5 %collective-permute-start.1 = (f32[8,96,96]{2,1,0:T(8,128)S(1)}, f32[8,96,96]{2,1,0:T(8,128)S(1)}, u32[]{:S(2)}, u32[]{:S(2)}) collective-permute-start(f32[8,96,96]{2,1,0:T(8,128)S(1)} %add_select_fusion.3), channel_id=1, source_target_pairs={{0,2},{1,3},{4,6},{5,7},{8,10},{9,11},{12,14},{13,15},{16,18},{17,... | collective-permute-start | bytes 884744 | tf_op jit(solution)/shard_map/ppermute | solution.py:392
  21.2 5.9 %all-to-all-start = ((bf16[8,32,768]{2,1,0:T(8,128)(2,1)}), bf16[8,32,768]{2,1,0:T(8,128)(2,1)S(1)}, u32[]{:S(2)}, u32[]{:S(2)}) async-start(bf16[8,32,768]{2,1,0:T(8,128)(2,1)} %turn.1), calls=%async_computation | async-start | bytes 786432 | tf_op jit(solution)/shard_map/all_to_all | solution.py:388
  47.9 3.2 %collective-permute-done.28 = f32[128,2]{0,1:T(2,128)S(1)} collective-permute-done((f32[128,2]{0,1:T(2,128)S(1)}, f32[128,2]{0,1:T(2,128)S(1)}, u32[]{:S(2)}, u32[]{:S(2)}) %collective-permute-start.28) | collective-permute-done | bytes 1056 | tf_op jit(solution)/shard_map/ppermute | solution.py:88
  60.2 10.0 %load_weights.1 = (bf16[1152,6144]{1,0:T(8,128)(2,1)S(1)}, bf16[1152,6144]{1,0:T(8,128)(2,1)S(1)}) custom-call(bf16[1152,6144]{1,0:T(8,128)(2,1)} %bitcast.206, bf16[1152,6144]{1,0:T(8,128)(2,1)} %bitcast.207, bf16[128,768]{1,0:T(8,128)(2,1)} %copy-done.27), custom_call_target="tpu_custom_call" | custom-call | tf_op jit(solution)/shard_map/load_weights/pallas_call | solution.py:154
  73.0 8.7 %collective-permute-done.8.refs_2_ = bf16[128,768]{1,0:T(8,128)(2,1)S(1)} collective-permute-done((bf16[128,768]{1,0:T(8,128)(2,1)S(1)}, bf16[128,768]{1,0:T(8,128)(2,1)S(1)}, u32[]{:S(2)}, u32[]{:S(2)}) %collective-permute-start.8) | collective-permute-done | bytes 196640 | tf_op jit(solution)/shard_map/ppermute | solution.py:81
  85.7 7.2 %collective-permute-done.16 = bf16[128,768]{1,0:T(8,128)(2,1)S(1)} collective-permute-done((bf16[128,768]{1,0:T(8,128)(2,1)S(1)}, bf16[128,768]{1,0:T(8,128)(2,1)S(1)}, u32[]{:S(2)}, u32[]{:S(2)}) %collective-permute-start.16) | collective-permute-done | bytes 196640 | tf_op jit(solution)/shard_map/ppermute | solution.py:84
  95.4 5.1 %collective-permute-done.9.refs_6_ = bf16[128,768]{1,0:T(8,128)(2,1)S(1)} collective-permute-done((bf16[128,768]{1,0:T(8,128)(2,1)S(1)}, bf16[128,768]{1,0:T(8,128)(2,1)S(1)}, u32[]{:S(2)}, u32[]{:S(2)}) %collective-permute-start.9) | collective-permute-done | bytes 196640 | tf_op jit(solution)/shard_map/ppermute | solution.py:81
  102.7 5.7 %collective-permute-done.17 = bf16[128,768]{1,0:T(8,128)(2,1)S(1)} collective-permute-done((bf16[128,768]{1,0:T(8,128)(2,1)S(1)}, bf16[128,768]{1,0:T(8,128)(2,1)S(1)}, u32[]{:S(2)}, u32[]{:S(2)}) %collective-permute-start.17) | collective-permute-done | bytes 196640 | tf_op jit(solution)/shard_map/ppermute | solution.py:88
  111.9 3.7 %before_rows.6 = (f32[512,1152]{1,0:T(8,128)S(1)}, f32[512,1]{1,0:T(8,128)S(1)}) custom-call(bf16[1152,6144]{1,0:T(8,128)(2,1)S(1)} %get-tuple-element.37.weight_ref, f32[8,768]{1,0:T(8,128)S(1)} %reshape.364.gain_ref, bf16[256,768]{1,0:T(8,128)(2,1)S(1)} %constant_dynamic-update-slice_fusion.10.refs_0_, ...), custom_call_target="tpu_custom_call" | custom-call | flops 1811939328 | bytes 3538944 | tf_op jit(solution)/shard_map/before_rows/pallas_call | solution.py:282
  115.5 3.6 %before_rows.7 = (f32[512,1152]{1,0:T(8,128)S(1)}, f32[512,1]{1,0:T(8,128)S(1)}) custom-call(bf16[1152,6144]{1,0:T(8,128)(2,1)S(1)} %get-tuple-element.37.weight_ref, f32[8,768]{1,0:T(8,128)S(1)} %reshape.364.gain_ref, bf16[256,768]{1,0:T(8,128)(2,1)S(1)} %constant_dynamic-update-slice_fusion.6.refs_0_, ...), custom_call_target="tpu_custom_call" | custom-call | flops 1811939328 | bytes 3538944 | tf_op jit(solution)/shard_map/before_rows/pallas_call | solution.py:282
  119.2 3.7 %before_rows.8 = (f32[512,1152]{1,0:T(8,128)S(1)}, f32[512,1]{1,0:T(8,128)S(1)}) custom-call(bf16[1152,6144]{1,0:T(8,128)(2,1)S(1)} %get-tuple-element.37.weight_ref, f32[8,768]{1,0:T(8,128)S(1)} %reshape.364.gain_ref, bf16[256,768]{1,0:T(8,128)(2,1)S(1)} %constant_dynamic-update-slice_fusion.2.refs_0_, ...), custom_call_target="tpu_custom_call" | custom-call | flops 1811939328 | bytes 3538944 | tf_op jit(solution)/shard_map/before_rows/pallas_call | solution.py:282
  126.6 3.1 %partial_rows.11 = (bf16[2,256,768]{2,1,0:T(8,128)(2,1)S(1)}, bf16[2,256,768]{2,1,0:T(8,128)(2,1)}) custom-call(bf16[1152,6144]{1,0:T(8,128)(2,1)S(1)} %get-tuple-element.38.weight_ref, bf16[512,1152]{1,0:T(8,128)(2,1)S(1)} %get-tuple-element.48.left_ref, f32[512,1]{1,0:T(8,128)S(1)} %copy.48.refs_4_.refs_0_.share_ref, ...), custom_call_target="tpu_custom_call" | custom-call | flops 1811939328 | bytes 3538944 | tf_op jit(solution)/shard_map/partial_rows/pallas_call | solution.py:320
  130.9 5.0 %copy-done.3 = bf16[1152,6144]{1,0:T(8,128)(2,1)S(1)} copy-done((bf16[1152,6144]{1,0:T(8,128)(2,1)S(1)}, bf16[1152,6144]{1,0:T(8,128)(2,1)}, u32[]{:S(2)}) %copy-start.3) | copy-done | bytes 14155800
  141.4 12.6 %backward_rows.1.left_ref = bf16[512,1152]{1,0:T(8,128)(2,1)S(1)} custom-call(bf16[512,6144]{1,0:T(8,128)(2,1)S(1)} %copy-done.7, bf16[1152,6144]{1,0:T(8,128)(2,1)S(1)} %copy-done.3, f32[512,1152]{1,0:T(8,128)S(1)} %copy-done.9, f32[512,1]{1,0:T(8,128)S(1)} %copy.48.refs_4_.refs_0_.share_ref, bf16[2,256,768]{2,1,0:T(8,128)(2,1)} %get-tuple-element.50.refs_0_, ...), custom_call_target="tpu_custom_call" | custom-call | flops 7247757312 | bytes 14155776 | tf_op jit(solution)/shard_map/backward_rows/pallas_call | solution.py:213
  154.0 5.0 %copy-done.1 = bf16[1152,6144]{1,0:T(8,128)(2,1)S(1)} copy-done((bf16[1152,6144]{1,0:T(8,128)(2,1)S(1)}, bf16[1152,6144]{1,0:T(8,128)(2,1)}, u32[]{:S(2)}) %copy-start.1) | copy-done | bytes 14155800
  183.1 7.3 %collective-permute-done.37.refs_2_ = bf16[2,128,768]{2,1,0:T(8,128)(2,1)S(1)} collective-permute-done((bf16[2,128,768]{2,1,0:T(8,128)(2,1)S(1)}, bf16[2,128,768]{2,1,0:T(8,128)(2,1)S(1)}, u32[]{:S(2)}, u32[]{:S(2)}) %collective-permute-start.37) | collective-permute-done | bytes 393248 | tf_op jit(solution)/shard_map/ppermute | solution.py:88
  194.5 3.9 %collective-permute-done.44 = bf16[128,768]{1,0:T(8,128)(2,1)S(1)} collective-permute-done((bf16[128,768]{1,0:T(8,128)(2,1)S(1)}, bf16[128,768]{1,0:T(8,128)(2,1)S(1)}, u32[]{:S(2)}, u32[]{:S(2)}) %collective-permute-start.44) | collective-permute-done | bytes 196640 | tf_op jit(solution)/shard_map/ppermute | solution.py:81
  202.4 3.4 %collective-permute-done.57 = bf16[256,768]{1,0:T(8,128)(2,1)S(1)} collective-permute-done((bf16[256,768]{1,0:T(8,128)(2,1)S(1)}, bf16[256,768]{1,0:T(8,128)(2,1)S(1)}, u32[]{:S(2)}, u32[]{:S(2)}) %collective-permute-start.57) | collective-permute-done | bytes 393248 | tf_op jit(solution)/shard_map/ppermute | solution.py:81
  210.5 11.1 %collective-permute-done.49 = bf16[128,768]{1,0:T(8,128)(2,1)S(1)} collective-permute-done((bf16[128,768]{1,0:T(8,128)(2,1)S(1)}, bf16[128,768]{1,0:T(8,128)(2,1)S(1)}, u32[]{:S(2)}, u32[]{:S(2)}) %collective-permute-start.49) | collective-permute-done | bytes 196640 | tf_op jit(solution)/shard_map/ppermute | solution.py:84
  233.4 5.3 %collective-permute-done.51 = f32[5,128]{1,0:T(8,128)S(1)} collective-permute-done((f32[5,128]{1,0:T(8,128)S(1)}, f32[5,128]{1,0:T(8,128)S(1)}, u32[]{:S(2)}, u32[]{:S(2)}) %collective-permute-start.51) | collective-permute-done | bytes 2592 | tf_op jit(solution)/shard_map/ppermute | solution.py:95
  238.8 3.6 %collective-permute-done.52 = f32[5,128]{1,0:T(8,128)S(1)} collective-permute-done((f32[5,128]{1,0:T(8,128)S(1)}, f32[5,128]{1,0:T(8,128)S(1)}, u32[]{:S(2)}, u32[]{:S(2)}) %collective-permute-start.52) | collective-permute-done | bytes 2592 | tf_op jit(solution)/shard_map/ppermute | solution.py:95
  247.0 5.2 %collective-permute-done.64 = bf16[128,768]{1,0:T(8,128)(2,1)S(1)} collective-permute-done((bf16[128,768]{1,0:T(8,128)(2,1)S(1)}, bf16[128,768]{1,0:T(8,128)(2,1)S(1)}, u32[]{:S(2)}, u32[]{:S(2)}) %collective-permute-start.64) | collective-permute-done | bytes 196640 | tf_op jit(solution)/shard_map/ppermute | solution.py:88
  259.4 3.5 %all-to-all-start.1 = ((bf16[8,32,768]{2,1,0:T(8,128)(2,1)}), bf16[8,32,768]{2,1,0:T(8,128)(2,1)S(1)}, u32[]{:S(2)}, u32[]{:S(2)}) async-start(bf16[8,32,768]{2,1,0:T(8,128)(2,1)} %pad_maximum_fusion.4), calls=%async_computation.1 | async-start | bytes 786432 | tf_op jit(solution)/shard_map/all_to_all | solution.py:501
  263.0 6.5 %collective-permute-done.66 = f32[8,96,96]{2,1,0:T(8,128)S(1)} collective-permute-done((f32[8,96,96]{2,1,0:T(8,128)S(1)}, f32[8,96,96]{2,1,0:T(8,128)S(1)}, u32[]{:S(2)}, u32[]{:S(2)}) %collective-permute-start.66) | collective-permute-done | bytes 294944 | tf_op jit(solution)/shard_map/ppermute | solution.py:508
  (324 shorter events, 131.2 us)
Async XLA Ops:
  7.2 123.8 %all-gather.2.cloned.1.call-start = ((), (), s32[]{:S(2)}) async-start(), calls=%async_computation.2 | async-start | bytes 6488064 | tf_op jit(solution)/shard_map/all_gather | solution.py:372
  13.8 14.9 %collective-permute-start.1 = (f32[8,96,96]{2,1,0:T(8,128)S(1)}, f32[8,96,96]{2,1,0:T(8,128)S(1)}, u32[]{:S(2)}, u32[]{:S(2)}) collective-permute-start(f32[8,96,96]{2,1,0:T(8,128)S(1)} %add_select_fusion.3), channel_id=1, source_target_pairs={{0,2},{1,3},{4,6},{5,7},{8,10},{9,11},{12,14},{13,15},{16,18},{17,... | collective-permute-start | bytes 884744 | tf_op jit(solution)/shard_map/ppermute | solution.py:392
  21.2 21.1 %all-to-all-start = ((bf16[8,32,768]{2,1,0:T(8,128)(2,1)}), bf16[8,32,768]{2,1,0:T(8,128)(2,1)S(1)}, u32[]{:S(2)}, u32[]{:S(2)}) async-start(bf16[8,32,768]{2,1,0:T(8,128)(2,1)} %turn.1), calls=%async_computation | async-start | bytes 786432 | tf_op jit(solution)/shard_map/all_to_all | solution.py:388
  52.5 40.7 %collective-permute-start.27 = (bf16[256,768]{1,0:T(8,128)(2,1)S(1)}, bf16[256,768]{1,0:T(8,128)(2,1)S(1)}, u32[]{:S(2)}, u32[]{:S(2)}) collective-permute-start(bf16[256,768]{1,0:T(8,128)(2,1)S(1)} %pad_maximum_fusion.refs_0_), channel_id=1, source_target_pairs={{0,1},{1,0},{2,3},{3,2},{4,5},{5,4},{6,7},{7,6},{8,9},{9,8},{10,11... | collective-permute-start | bytes 1179656 | tf_op jit(solution)/shard_map/ppermute | solution.py:88
  54.1 16.8 %collective-permute-start.7 = (bf16[128,768]{1,0:T(8,128)(2,1)S(1)}, bf16[128,768]{1,0:T(8,128)(2,1)S(1)}, u32[]{:S(2)}, u32[]{:S(2)}) collective-permute-start(bf16[128,768]{1,0:T(8,128)(2,1)S(1)} %collective-permute-done.6), channel_id=1, source_target_pairs={{0,8},{8,16},{16,24},{24,28},{28,20},{20,12},{12,4},{4,0},{1,9},{9... | collective-permute-start | bytes 589832 | tf_op jit(solution)/shard_map/ppermute | solution.py:81
  54.3 16.0 %collective-permute-start.23 = (bf16[128,768]{1,0:T(8,128)(2,1)S(1)}, bf16[128,768]{1,0:T(8,128)(2,1)S(1)}, u32[]{:S(2)}, u32[]{:S(2)}) collective-permute-start(bf16[128,768]{1,0:T(8,128)(2,1)S(1)} %collective-permute-done.6), channel_id=1, source_target_pairs={{0,2},{1,3},{2,0},{3,1},{4,6},{5,7},{6,4},{7,5},{8,10},{9,11},{10,... | collective-permute-start | bytes 589832 | tf_op jit(solution)/shard_map/ppermute | solution.py:88
  56.8 13.6 %collective-permute-start.25 = (bf16[128,768]{1,0:T(8,128)(2,1)S(1)}, bf16[128,768]{1,0:T(8,128)(2,1)S(1)}, u32[]{:S(2)}, u32[]{:S(2)}) collective-permute-start(bf16[128,768]{1,0:T(8,128)(2,1)S(1)} %collective-permute-done.14), channel_id=1, source_target_pairs={{0,2},{1,3},{2,0},{3,1},{4,6},{5,7},{6,4},{7,5},{8,10},{9,11},{10,... | collective-permute-start | bytes 589832 | tf_op jit(solution)/shard_map/ppermute | solution.py:88
  70.3 38.0 %collective-permute-start.24 = (bf16[256,768]{1,0:T(8,128)(2,1)S(1)}, bf16[256,768]{1,0:T(8,128)(2,1)S(1)}, u32[]{:S(2)}, u32[]{:S(2)}) collective-permute-start(bf16[256,768]{1,0:T(8,128)(2,1)S(1)} %constant_dynamic-update-slice_fusion.10.refs_0_), channel_id=1, source_target_pairs={{0,1},{1,0},{2,3},{3,2},{4,5},{5,4},{6,7},{7,6},{8,9},{9,8},{10,11... | collective-permute-start | bytes 1179656 | tf_op jit(solution)/shard_map/ppermute | solution.py:88
  70.4 40.9 %collective-permute-start.26 = (bf16[256,768]{1,0:T(8,128)(2,1)S(1)}, bf16[256,768]{1,0:T(8,128)(2,1)S(1)}, u32[]{:S(2)}, u32[]{:S(2)}) collective-permute-start(bf16[256,768]{1,0:T(8,128)(2,1)S(1)} %constant_dynamic-update-slice_fusion.12.refs_2_), channel_id=1, source_target_pairs={{0,1},{1,0},{2,3},{3,2},{4,5},{5,4},{6,7},{7,6},{8,9},{9,8},{10,11... | collective-permute-start | bytes 1179656 | tf_op jit(solution)/shard_map/ppermute | solution.py:88
  92.9 22.6 %collective-permute-start.20 = (bf16[256,768]{1,0:T(8,128)(2,1)S(1)}, bf16[256,768]{1,0:T(8,128)(2,1)S(1)}, u32[]{:S(2)}, u32[]{:S(2)}) collective-permute-start(bf16[256,768]{1,0:T(8,128)(2,1)S(1)} %constant_dynamic-update-slice_fusion.6.refs_0_), channel_id=1, source_target_pairs={{0,1},{1,0},{2,3},{3,2},{4,5},{5,4},{6,7},{7,6},{8,9},{9,8},{10,11... | collective-permute-start | bytes 1179656 | tf_op jit(solution)/shard_map/ppermute | solution.py:88
  129.7 30.8 %collective-permute-start.31 = (bf16[2,256,768]{2,1,0:T(8,128)(2,1)}, bf16[2,256,768]{2,1,0:T(8,128)(2,1)S(1)}, u32[]{:S(2)}, u32[]{:S(2)}) collective-permute-start(bf16[2,256,768]{2,1,0:T(8,128)(2,1)} %get-tuple-element.50.refs_0_), channel_id=1, source_target_pairs={{0,1},{1,0},{2,3},{3,2},{4,5},{5,4},{6,7},{7,6},{8,9},{9,8},{10,11... | collective-permute-start | bytes 2359304 | tf_op jit(solution)/shard_map/ppermute | solution.py:88
  164.1 26.9 %collective-permute-start.56 = (bf16[128,768]{1,0:T(8,128)(2,1)S(1)}, bf16[128,768]{1,0:T(8,128)(2,1)S(1)}, u32[]{:S(2)}, u32[]{:S(2)}) collective-permute-start(bf16[128,768]{1,0:T(8,128)(2,1)S(1)} %get-tuple-element.109), channel_id=1, source_target_pairs={{0,8},{8,16},{16,24},{24,28},{28,20},{20,12},{12,4},{4,0},{1,9},{9... | collective-permute-start | bytes 589832 | tf_op jit(solution)/shard_map/ppermute | solution.py:81
  164.6 28.0 %collective-permute-start.60 = (bf16[128,768]{1,0:T(8,128)(2,1)S(1)}, bf16[128,768]{1,0:T(8,128)(2,1)S(1)}, u32[]{:S(2)}, u32[]{:S(2)}) collective-permute-start(bf16[128,768]{1,0:T(8,128)(2,1)S(1)} %get-tuple-element.110), channel_id=1, source_target_pairs={{8,0},{16,8},{24,16},{28,24},{20,28},{12,20},{4,12},{0,4},{9,1},{1... | collective-permute-start | bytes 589832 | tf_op jit(solution)/shard_map/ppermute | solution.py:84
  181.2 19.4 %collective-permute-start.38 = (bf16[2,256,768]{2,1,0:T(8,128)(2,1)S(1)}, bf16[2,256,768]{2,1,0:T(8,128)(2,1)S(1)}, u32[]{:S(2)}, u32[]{:S(2)}) collective-permute-start(bf16[2,256,768]{2,1,0:T(8,128)(2,1)S(1)} %get-tuple-element.57.refs_1_), channel_id=1, source_target_pairs={{0,1},{1,0},{2,3},{3,2},{4,5},{5,4},{6,7},{7,6},{8,9},{9,8},{10,11... | collective-permute-start | bytes 2359304 | tf_op jit(solution)/shard_map/ppermute | solution.py:88
  181.3 17.2 %collective-permute-start.42 = (bf16[2,128,768]{2,1,0:T(8,128)(2,1)S(1)}, bf16[2,128,768]{2,1,0:T(8,128)(2,1)S(1)}, u32[]{:S(2)}, u32[]{:S(2)}) collective-permute-start(bf16[2,128,768]{2,1,0:T(8,128)(2,1)S(1)} %pad_maximum_fusion.3), channel_id=1, source_target_pairs={{0,2},{1,3},{2,0},{3,1},{4,6},{5,7},{6,4},{7,5},{8,10},{9,11},{10,... | collective-permute-start | bytes 1179656 | tf_op jit(solution)/shard_map/ppermute | solution.py:88
  198.5 25.8 %collective-permute-start.55 = (bf16[2,256,768]{2,1,0:T(8,128)(2,1)S(1)}, bf16[2,256,768]{2,1,0:T(8,128)(2,1)S(1)}, u32[]{:S(2)}, u32[]{:S(2)}) collective-permute-start(bf16[2,256,768]{2,1,0:T(8,128)(2,1)S(1)} %get-tuple-element.56.refs_0_), channel_id=1, source_target_pairs={{0,1},{1,0},{2,3},{3,2},{4,5},{5,4},{6,7},{7,6},{8,9},{9,8},{10,11... | collective-permute-start | bytes 2359304 | tf_op jit(solution)/shard_map/ppermute | solution.py:88
  205.8 15.8 %collective-permute-start.41 = (bf16[2,128,768]{2,1,0:T(8,128)(2,1)S(1)}, bf16[2,128,768]{2,1,0:T(8,128)(2,1)S(1)}, u32[]{:S(2)}, u32[]{:S(2)}) collective-permute-start(bf16[2,128,768]{2,1,0:T(8,128)(2,1)S(1)} %pad_maximum_fusion.2), channel_id=1, source_target_pairs={{0,2},{1,3},{2,0},{3,1},{4,6},{5,7},{6,4},{7,5},{8,10},{9,11},{10,... | collective-permute-start | bytes 1179656 | tf_op jit(solution)/shard_map/ppermute | solution.py:88
  206.5 15.7 %collective-permute-start.58 = (bf16[256,768]{1,0:T(8,128)(2,1)S(1)}, bf16[256,768]{1,0:T(8,128)(2,1)S(1)}, u32[]{:S(2)}, u32[]{:S(2)}) collective-permute-start(bf16[256,768]{1,0:T(8,128)(2,1)S(1)} %get-tuple-element.93), channel_id=1, source_target_pairs={{0,8},{8,16},{16,24},{24,28},{28,20},{20,12},{12,4},{4,0},{1,9},{9... | collective-permute-start | bytes 1179656 | tf_op jit(solution)/shard_map/ppermute | solution.py:81
  210.0 14.0 %collective-permute-start.62 = (bf16[256,768]{1,0:T(8,128)(2,1)S(1)}, bf16[256,768]{1,0:T(8,128)(2,1)S(1)}, u32[]{:S(2)}, u32[]{:S(2)}) collective-permute-start(bf16[256,768]{1,0:T(8,128)(2,1)S(1)} %get-tuple-element.94), channel_id=1, source_target_pairs={{8,0},{16,8},{24,16},{28,24},{20,28},{12,20},{4,12},{0,4},{9,1},{1... | collective-permute-start | bytes 1179656 | tf_op jit(solution)/shard_map/ppermute | solution.py:84
  221.6 23.6 %collective-permute-start.54 = (bf16[1,256,768]{2,1,0:T(8,128)(2,1)S(1)}, bf16[1,256,768]{2,1,0:T(8,128)(2,1)S(1)}, u32[]{:S(2)}, u32[]{:S(2)}) collective-permute-start(bf16[1,256,768]{2,1,0:T(8,128)(2,1)S(1)} %get-tuple-element.59.refs_0_), channel_id=1, source_target_pairs={{0,1},{1,0},{2,3},{3,2},{4,5},{5,4},{6,7},{7,6},{8,9},{9,8},{10,11... | collective-permute-start | bytes 1179656 | tf_op jit(solution)/shard_map/ppermute | solution.py:88
  224.6 20.6 %collective-permute-start.59 = (bf16[256,768]{1,0:T(8,128)(2,1)S(1)}, bf16[256,768]{1,0:T(8,128)(2,1)S(1)}, u32[]{:S(2)}, u32[]{:S(2)}) collective-permute-start(bf16[256,768]{1,0:T(8,128)(2,1)S(1)} %get-tuple-element.91), channel_id=1, source_target_pairs={{0,8},{8,16},{16,24},{24,28},{28,20},{20,12},{12,4},{4,0},{1,9},{9... | collective-permute-start | bytes 1179656 | tf_op jit(solution)/shard_map/ppermute | solution.py:81
  228.9 16.2 %collective-permute-start.63 = (bf16[256,768]{1,0:T(8,128)(2,1)S(1)}, bf16[256,768]{1,0:T(8,128)(2,1)}, u32[]{:S(2)}, u32[]{:S(2)}) collective-permute-start(bf16[256,768]{1,0:T(8,128)(2,1)S(1)} %get-tuple-element.92), channel_id=1, source_target_pairs={{8,0},{16,8},{24,16},{28,24},{20,28},{12,20},{4,12},{0,4},{9,1},{1... | collective-permute-start | bytes 1179656 | tf_op jit(solution)/shard_map/ppermute | solution.py:84
  256.5 13.1 %collective-permute-start.66 = (f32[8,96,96]{2,1,0:T(8,128)S(1)}, f32[8,96,96]{2,1,0:T(8,128)S(1)}, u32[]{:S(2)}, u32[]{:S(2)}) collective-permute-start(f32[8,96,96]{2,1,0:T(8,128)S(1)} %add_select_fusion.1), channel_id=1, source_target_pairs={{2,0},{3,1},{6,4},{7,5},{10,8},{11,9},{14,12},{15,13},{18,16},{19,... | collective-permute-start | bytes 884744 | tf_op jit(solution)/shard_map/ppermute | solution.py:508
  259.4 15.6 %all-to-all-start.1 = ((bf16[8,32,768]{2,1,0:T(8,128)(2,1)}), bf16[8,32,768]{2,1,0:T(8,128)(2,1)S(1)}, u32[]{:S(2)}, u32[]{:S(2)}) async-start(bf16[8,32,768]{2,1,0:T(8,128)(2,1)} %pad_maximum_fusion.4), calls=%async_computation.1 | async-start | bytes 786432 | tf_op jit(solution)/shard_map/all_to_all | solution.py:501
  (91 other events, 1120.1 us)
Sparse Core Ops, SparseCore 0:
  11.0 82.4 all-gather.1
where the time goes:
time: 288 us; the launch traced here: 283 us
  waiting for transfers between devices  101 us (35%)
  starting transfers between devices  66.9 us (23%)
  Pallas kernels  58.3 us (20%)
  local copies, waits for them, and re-layouts  27.7 us (10%)
  between operations  15.5 us (5%)
  other arithmetic  7.84 us (3%)
  matrix products  6.23 us (2%)
    ppermute x36, waiting for transfers between devices, swap(): lax.ppermute(x, 'exp', [(i, i ^ k) for i in range(lax.axis_size('exp'))])  30.9 us
    ppermute x12, waiting for transfers between devices, go_right(): return lax.ppermute(x, 'ctx', self.right)  25.5 us
    unnamed x104, local copies, waits for them, and re-layouts  23.3 us
    ppermute x36, starting transfers between devices, swap(): lax.ppermute(x, 'exp', [(i, i ^ k) for i in range(lax.axis_size('exp'))])  20.3 us
    ppermute x11, waiting for transfers between devices, go_left(): return lax.ppermute(x, 'ctx', self.left)  19.3 us
    pallas_call x10, Pallas kernels, second_call(): pl.pallas_call(kernel, in_specs=[WHOLE] * (2 + len(extra)) + [ANYWHERE] *...  19.1 us
    pallas_call x5, Pallas kernels, before_call(): pl.pallas_call(kernel, in_specs=[WHOLE, WHOLE] + [ANYWHERE] * len(pieces)...  14.8 us
    ppermute x6, waiting for transfers between devices, ctx_sum(): x = x + lax.ppermute(x, 'ctx', [(i, i ^ step) for i in range(size)])  14.1 us
  transfers between devices with their start and end apart: 70, of which 28 were waited for; matrix products, arithmetic and copies ran while one was open for 7% of the time, Pallas kernels for 21%

commit v1 on v0

--- a/solution.py
+++ b/solution.py
@@ -97,14 +97,17 @@
     return x
 
 
-def ring_sum(partial, ring):
-    far = partial[4]
-    rows = far.shape[0]
+def ring_start(far, ring):
     low = far.astype(BF16)
-    to_right, to_left = low[: rows // 2], low[rows // 2 :]
+    half = low.shape[0] // 2
+    return ring.go_right(low[:half]), ring.go_left(low[half:])
+
+
+def ring_sum(partial, start, ring):
+    to_right, to_left = start
     blank = jnp.zeros_like(to_right)
-    to_right = jnp.concatenate([ring.go_right(to_right), blank], axis=0)
-    to_left = jnp.concatenate([blank, ring.go_left(to_left)], axis=0)
+    to_right = jnp.concatenate([to_right, blank], axis=0)
+    to_left = jnp.concatenate([blank, to_left], axis=0)
     for offset in (3, 2, 1):
         to_right = ring.go_right((partial[offset] + to_right.astype(F32)).astype(BF16))
         to_left = ring.go_left((partial[-offset] + to_left.astype(F32)).astype(BF16))
@@ -137,39 +140,28 @@
     )
 
 
-def load_call(arrays, after=()):
-    count = len(arrays)
-
+def meet(*arrays):
     def kernel(*refs):
-        sources, targets, arrived = refs[:count], refs[-1 - count : -1], refs[-1]
-        copies = [
-            pltpu.make_async_copy(source, target, arrived.at[k])
-            for k, (source, target) in enumerate(zip(sources, targets))
-        ]
-        for copy in copies:
-            copy.start()
-        for copy in copies:
-            copy.wait()
+        pass
 
     return pl.pallas_call(
         kernel,
-        in_specs=[IN_HBM] * count + [ANYWHERE] * len(after),
-        out_specs=[WHOLE] * count,
-        out_shape=[pltpu.VMEM(x.shape, x.dtype) for x in arrays],
-        scratch_shapes=[pltpu.SemaphoreType.DMA((count,))],
-        compiler_params=pltpu.CompilerParams(vmem_limit_bytes=32 * 2**20),
-        name="load_weights",
-    )(*arrays, *after)
-
-
-def backward_call(rows_all, weight, before, share, after=()):
+        in_specs=[ANYWHERE] * len(arrays),
+        out_specs=[ANYWHERE] * len(arrays),
+        out_shape=[jax.ShapeDtypeStruct(x.shape, x.dtype) for x in arrays],
+        input_output_aliases={k: k for k in range(len(arrays))},
+        name="meet",
+    )(*arrays)
+
+
+def backward_call(rows_all, weight, after=()):
     rows, features = rows_all.shape
     hidden = weight.shape[0]
     span, parts = rows // 4, 4
     part = features // parts
 
-    def kernel(rows_ref, weight_ref, before_ref, share_ref, *refs):
-        out_ref, held, total, landed = refs[-4:]
+    def kernel(rows_ref, weight_ref, *refs):
+        total, held, landed = refs[-3:]
         mine = lax.axis_index("exp")
         core, side = lax.rem(mine, 2), mine // 2
 
@@ -205,59 +197,55 @@
                 preferred_element_type=F32,
             )
             total[...] = value if k == 0 else total[...] + value
-        here, share = before_ref[...], share_ref[...]
-        sigma = 1.0 / (1.0 + jnp.exp(-here))
-        value = share * total[...] * (sigma * (1.0 + here * (1.0 - sigma)))
-        out_ref[...] = jnp.where(share > 0.0, value, 0.0).astype(BF16)
 
     return pl.pallas_call(
         kernel,
-        in_specs=[IN_HBM] + [WHOLE] * 3 + [ANYWHERE] * len(after),
+        in_specs=[IN_HBM, WHOLE] + [ANYWHERE] * len(after),
         out_specs=WHOLE,
-        out_shape=jax.ShapeDtypeStruct((rows, hidden), BF16),
+        out_shape=jax.ShapeDtypeStruct((rows, hidden), F32),
         scratch_shapes=[
             pltpu.VMEM((2, rows, part), BF16),
-            pltpu.VMEM((rows, hidden), F32),
             pltpu.SemaphoreType.DMA((2, 4)),
         ],
         compiler_params=pltpu.CompilerParams(vmem_limit_bytes=10 * 2**20),
         cost_estimate=cost(rows, hidden, features),
         name="backward_rows",
-    )(rows_all, weight, before, share, *after)
-
-
-def before_call(found, ring, offsets, weight, gain, start=None, share=None, after=()):
+    )(rows_all, weight, *after)
+
+
+def before_call(found, ring, offsets, weight, gain, start=None, finish=None, after=()):
     count = len(offsets)
     pieces = [part for o in offsets for part in found[o]]
-    half, width = pieces[0].shape
-    rows, hidden, features, size = 2 * half, weight.shape[0], weight.shape[1], ring.size
+    span, width = pieces[0].shape
+    rows, hidden, features, size = 4 * span, weight.shape[0], weight.shape[1], ring.size
     gain = gain.reshape(size, width)
     sums = [jax.ShapeDtypeStruct((rows, hidden), F32), jax.ShapeDtypeStruct((rows, 1), F32)]
-    first, last = start is None, share is not None
+    first, last = start is None, finish is not None
 
     def kernel(weight_ref, gain_ref, *refs):
         refs = list(refs)
         parts = [refs.pop(0) for _ in pieces]
         begin = [] if first else [refs.pop(0), refs.pop(0)]
-        share_ref = refs.pop(0) if last else None
+        ending = [refs.pop(0), refs.pop(0)] if last else []
         refs = refs[len(after) :]
-        total, other = refs.pop(0), refs.pop(0)
+        outs = [refs.pop(0), refs.pop(0)]
         held, scaled, landed = refs[:3]
+        total = refs[3] if last else outs[0]
         copies = []
         for k in range(count):
-            for side in range(2):
+            for j in range(4):
                 copies.append(
                     pltpu.make_async_copy(
-                        parts[2 * k + side],
-                        held.at[k, pl.ds(side * half, half), :],
-                        landed.at[2 * k + side],
+                        parts[4 * k + j],
+                        held.at[k, pl.ds(j * span, span), :],
+                        landed.at[4 * k + j],
                     )
                 )
                 copies[-1].start()
         square = None if first else begin[1][...]
         for k in range(count):
-            copies[2 * k].wait()
-            copies[2 * k + 1].wait()
+            for copy in copies[4 * k : 4 * k + 4]:
+                copy.wait()
             value = held[k].astype(F32)
             squares = jnp.sum(value * value, axis=-1, keepdims=True)
             square = squares if square is None else square + squares
@@ -272,13 +260,19 @@
                 total[...] += product
         if last:
             before = total[...] * lax.rsqrt(square / features + EPSILON)
-            total[...] = before
-            active = before * (1.0 / (1.0 + jnp.exp(-before)))
-            other[...] = jnp.where(share_ref[...] > 0.0, active, 0.0).astype(BF16)
+            sigma = 1.0 / (1.0 + jnp.exp(-before))
+            backward_ref, share_ref = ending
+            share = share_ref[...]
+            routed = share > 0.0
+            outs[0][...] = jnp.where(routed, before * sigma, 0.0).astype(BF16)
+            slope = sigma * (1.0 + before * (1.0 - sigma))
+            inner = share * backward_ref[...] * slope
+            outs[1][...] = jnp.where(routed, inner, 0.0).astype(BF16)
         else:
-            other[...] = square
-
-    rest = list(start or ()) + ([share] if last else [])
+            outs[1][...] = square
+
+    rest = list(start or ()) + list(finish or ())
+    lows = [jax.ShapeDtypeStruct((rows, hidden), BF16)] * 2
     return pl.pallas_call(
         kernel,
         in_specs=[WHOLE, WHOLE]
@@ -286,13 +280,14 @@
         + [WHOLE] * len(rest)
         + [ANYWHERE] * len(after),
         out_specs=[WHOLE, WHOLE],
-        out_shape=[sums[0], jax.ShapeDtypeStruct((rows, hidden), BF16) if last else sums[1]],
+        out_shape=lows if last else sums,
         scratch_shapes=[
             pltpu.VMEM((count, rows, width), BF16),
             pltpu.VMEM((rows, width), BF16),
-            pltpu.SemaphoreType.DMA((2 * count,)),
-        ],
-        compiler_params=pltpu.CompilerParams(vmem_limit_bytes=8 * 2**20),
+            pltpu.SemaphoreType.DMA((4 * count,)),
+        ]
+        + ([pltpu.VMEM((rows, hidden), F32)] if last else []),
+        compiler_params=pltpu.CompilerParams(vmem_limit_bytes=10 * 2**20),
         cost_estimate=cost(rows, hidden, count * width),
         name="before_rows",
     )(weight, gain, *pieces, *rest, *after)
@@ -328,11 +323,12 @@
     )(weight, left, *extra, *after)
 
 
-def turn_call(residual, cotangent, after, ring):
+def turn_call(residual, cotangent, ring, after):
     rows, features = residual.shape
     width = features // ring.size
 
-    def kernel(residual_ref, cotangent_ref, after_ref, out_ref):
+    def kernel(residual_ref, cotangent_ref, *refs):
+        out_ref = refs[-1]
         for k in range(ring.size):
             span = pl.ds(k * width, width)
             out_ref[k, pl.ds(0, rows), :] = residual_ref[:, span]
@@ -340,11 +336,11 @@
 
     return pl.pallas_call(
         kernel,
-        in_specs=[WHOLE, WHOLE, ANYWHERE],
+        in_specs=[WHOLE, WHOLE] + [ANYWHERE] * len(after),
         out_specs=WHOLE,
         out_shape=jax.ShapeDtypeStruct((ring.size, 2 * rows, width), BF16),
         name="turn",
-    )(residual, cotangent, after)
+    )(residual, cotangent, *after)
 
 
 def fast_device(
@@ -384,7 +380,7 @@
     summary = jax.vmap(span_summary, in_axes=(1, 1, 0))(key_heads, value_heads, decay_slopes)
     other = swap(summary, 1)
     pair = jnp.where(core == 0, fade * summary + other, fade * other + summary)
-    both = turn_call(residual, cotangent, other, ring)
+    both = turn_call(residual, cotangent, ring, (other, share))
     both = lax.all_to_all(both, "ctx", split_axis=0, concat_axis=0, tiled=True)
     both = both.reshape(ring.size, 2, -1, width)
     residual_part = both[:, 0].reshape(length, width)
@@ -405,10 +401,11 @@
     hidden = hidden_low.astype(F32)
     across = swap(hidden_low, 2)
     rights, lefts = [hidden_low], [hidden_low]
-    for step in range(1, 5):
-        rights.append(ring.go_right(rights[-1]))
-        if step < 4:
-            lefts.append(ring.go_left(lefts[-1]))
+    for step in range(1, 4):
+        right, left = meet(ring.go_right(rights[-1]), ring.go_left(lefts[-1]))
+        rights.append(right)
+        lefts.append(left)
+    rights.append(ring.go_right(rights[-1]))
     cot = cot_part.astype(F32)
     early = jnp.stack(
         [
@@ -418,23 +415,25 @@
         ]
     )
 
-    up_hidden, down_hidden = load_call((up_weight[0], down_weight[0]), (across,))
+    up_hidden = up_weight[0]
     found = {}
     for step in range(5):
         for offset, rows in ((-step, rights), (step, lefts)):
             if (step < 4 and (step > 0 or rows is rights)) or (step == 4 and rows is rights):
                 own = rows[step]
-                own = jnp.concatenate([own, across if step == 0 else swap(own, 2)], axis=0)
-                found[4 if step == 4 else offset] = (own, swap(own, 1))
-
-    def before_part(offsets, sums=None, share=None, after=()):
-        return before_call(found, ring, offsets, up_hidden, expert_gain, sums, share, after)
+                far = across if step == 0 else swap(own, 2)
+                found[4 if step == 4 else offset] = (own, far, swap(own, 1), swap(far, 1))
+
+    def before_part(offsets, sums=None, finish=None, after=()):
+        return before_call(found, ring, offsets, up_hidden, expert_gain, sums, finish, after)
 
     sums = before_part((0,), after=(rights[3],))
-    sums = before_part((-1, 1), sums, after=(rights[4],))
+    down_hidden = down_weight[0]
+    backward = backward_call(cot_all, down_hidden, (rights[4], sums[1]))
+    sums = before_part((-1, 1), sums, after=(backward,))
     sums = before_part((-2, 2), sums)
     sums = before_part((-3, 3), sums)
-    before, active = before_part((4,), sums, share)
+    active, inner_grad = before_part((4,), sums, (backward, share))
 
     in_parts, out_parts = {}, {}
 
@@ -458,24 +457,24 @@
             in_parts[o] = in_parts[o][:length] + far[i].astype(F32)
         return far
 
-    give, got_a = second_out((4,))
-    give, got_b = second_out((3, -3), give)
-    inner_grad = backward_call(cot_all, down_hidden, before, share, (give, got_a))
-    give, got_c = second_in((4,))
-    far_0 = cross((4,))
-    give, got_d = second_in((3, -3), give, got_b)
-    far_1 = cross((3, -3))
-    give, got_e = second_out((2, -2), give, got_c)
-    give, got_f = second_in((2, -2), give, got_d)
-    cross((2, -2))
-    give, _ = second_out((1, -1), give, got_e, far_0)
-    give, got_g = second_in((1, -1), give, got_f)
+    give, got_in_4 = second_in((4,))
+    far_4 = cross((4,))
+    give, got_out_4 = second_out((4,), give)
+    out_start = ring_start(out_parts[4], ring)
+    give, got_in_3 = second_in((3, -3), give)
+    far_3 = cross((3, -3))
+    give, got_out_3 = second_out((3, -3), give, got_in_4)
+    give, got_in_2 = second_in((2, -2), give, got_out_4)
+    far_2 = cross((2, -2))
+    give, got_out_2 = second_out((2, -2), give, got_in_3)
+    give, got_in_1 = second_in((1, -1), give, got_out_3, far_4)
     cross((1, -1))
-    give, _ = second_out((0,), give, far_1)
-    second_in((0,), give, got_g)
+    give, _ = second_out((1, -1), give, got_in_2, *out_start)
+    give, _ = second_in((0,), give, far_3)
     cross((0,))
-    collected = ring_sum(in_parts, ring)
-    combined = ring_sum(out_parts, ring)
+    second_out((0,), give, got_out_2, far_2)
+    collected = ring_sum(in_parts, ring_start(in_parts[4], ring), ring)
+    combined = ring_sum(out_parts, out_start, ring)
     combined = combined[:length] + swap(combined[length:].astype(BF16), 2).astype(F32)
 
     gained = exp_gain * collected

time: 288 us -> 272 us (0.944)
  waiting for transfers between devices: 101 us -> 74.4 us
  starting transfers between devices: 66.9 us -> 77.8 us
  Pallas kernels: 58.3 us -> 50.9 us
  local copies, waits for them, and re-layouts: 27.7 us -> 34.6 us
    pallas_call x3 -> x5, Pallas kernels: 24.4 us -> 13.6 us  [the longest x1 11.8 us: backward_call(): pl.pallas_call(kernel, in_specs=[IN_HBM, WHOLE] + [ANYWHERE] * len(after)...]
    ppermute x12, waiting for transfers between devices: 25.5 us -> 15.1 us  [go_right(): return lax.ppermute(x, 'ctx', self.right)]
    ppermute x36 -> x44, waiting for transfers between devices: 30.9 us -> 21.7 us  [swap(): lax.ppermute(x, 'exp', [(i, i ^ k) for i in range(lax.axis_size('exp'))])]
    unnamed x104 -> x123, local copies, waits for them, and re-layouts: 23.3 us -> 30.2 us
    ppermute x11, waiting for transfers between devices: 19.3 us -> 12.5 us  [go_left(): return lax.ppermute(x, 'ctx', self.left)]
    ppermute x36 -> x44, starting transfers between devices: 20.3 us -> 27 us  [swap(): lax.ppermute(x, 'exp', [(i, i ^ k) for i in range(lax.axis_size('exp'))])]
    ppermute x12, starting transfers between devices: 9.99 us -> 15.3 us  [go_right(): return lax.ppermute(x, 'ctx', self.right)]
    pallas_call x5, Pallas kernels: 14.8 us -> 19 us  [before_call(): pl.pallas_call(kernel, in_specs=[WHOLE, WHOLE] + [ANYWHERE] * len(pieces)...]
  transfers between devices with their start and end apart: 70 -> 78, of which waited for: 28 -> 30; matrix products, arithmetic and copies ran while one was open for 7% -> 8% of each run, Pallas kernels for 21% -> 17%
where the time goes in v1:
time: 272 us; the launch traced here: 267 us
  starting transfers between devices  77.8 us (29%)
  waiting for transfers between devices  74.4 us (27%)
  Pallas kernels  50.9 us (19%)
  local copies, waits for them, and re-layouts  34.6 us (13%)
  between operations  15.4 us (6%)
  other arithmetic  7.7 us (3%)
  matrix products  6.25 us (2%)
    unnamed x123, local copies, waits for them, and re-layouts  30.2 us
    ppermute x44, starting transfers between devices, swap(): lax.ppermute(x, 'exp', [(i, i ^ k) for i in range(lax.axis_size('exp'))])  27 us
    ppermute x44, waiting for transfers between devices, swap(): lax.ppermute(x, 'exp', [(i, i ^ k) for i in range(lax.axis_size('exp'))])  21.7 us
    pallas_call x5, Pallas kernels, before_call(): pl.pallas_call(kernel, in_specs=[WHOLE, WHOLE] + [ANYWHERE] * len(pieces)...  19 us
    pallas_call x10, Pallas kernels, second_call(): pl.pallas_call(kernel, in_specs=[WHOLE] * (2 + len(extra)) + [ANYWHERE] *...  18.3 us
    ppermute x6, waiting for transfers between devices, ctx_sum(): x = x + lax.ppermute(x, 'ctx', [(i, i ^ step) for i in range(size)])  15.4 us
    ppermute x12, starting transfers between devices, go_right(): return lax.ppermute(x, 'ctx', self.right)  15.3 us
    ppermute x12, waiting for transfers between devices, go_right(): return lax.ppermute(x, 'ctx', self.right)  15.1 us
  transfers between devices with their start and end apart: 78, of which 30 were waited for; matrix products, arithmetic and copies ran while one was open for 8% of the time, Pallas kernels for 17%

profile of v1, /device:TPU:0, one launch (start us, length us, event | category | flops | bytes accessed | tf_op | source)
XLA Modules:
  0.0 267.0 jit_solution(9605046759031365495)
XLA Ops:
  12.7 2.5 collective-permute-start.1
  23.6 6.3 %all-to-all-start = ((bf16[8,32,768]{2,1,0:T(8,128)(2,1)}), bf16[8,32,768]{2,1,0:T(8,128)(2,1)S(1)}, u32[]{:S(2)}, u32[]{:S(2)}) async-start(bf16[8,32,768]{2,1,0:T(8,128)(2,1)} %turn.1), calls=%async_computation | async-start | bytes 786432 | tf_op jit(solution)/shard_map/all_to_all | solution.py:384
  39.2 2.8 %collective-permute-start.6 = (f32[1,128]{1,0:T(1,128)S(1)}, f32[1,128]{1,0:T(1,128)S(1)}, u32[]{:S(2)}, u32[]{:S(2)}) collective-permute-start(f32[1,128]{1,0:T(1,128)S(1)} %add.313), channel_id=1, source_target_pairs={{0,16},{4,20},{8,24},{12,28},{16,0},{20,4},{24,8},{28,12},{1,17},{... | collective-permute-start | bytes 1544 | tf_op jit(solution)/shard_map/ppermute | solution.py:95
  46.6 2.6 collective-permute-start.35
  49.2 4.4 %collective-permute-done.7.refs_0_ = bf16[128,768]{1,0:T(8,128)(2,1)S(1)} collective-permute-done((bf16[128,768]{1,0:T(8,128)(2,1)S(1)}, bf16[128,768]{1,0:T(8,128)(2,1)S(1)}, u32[]{:S(2)}, u32[]{:S(2)}) %collective-permute-start.7) | collective-permute-done | bytes 196640 | tf_op jit(solution)/shard_map/ppermute | solution.py:81
  69.0 8.0 %collective-permute-done.32.refs_5_ = bf16[128,768]{1,0:T(8,128)(2,1)S(1)} collective-permute-done((bf16[128,768]{1,0:T(8,128)(2,1)}, bf16[128,768]{1,0:T(8,128)(2,1)S(1)}, u32[]{:S(2)}, u32[]{:S(2)}) %collective-permute-start.32) | collective-permute-done | bytes 196640 | tf_op jit(solution)/shard_map/ppermute | solution.py:88
  78.1 2.4 collective-permute-start.23
  86.6 5.5 %copy-done = bf16[1,1152,6144]{2,1,0:T(8,128)(2,1)S(1)} copy-done((bf16[1,1152,6144]{2,1,0:T(8,128)(2,1)S(1)}, bf16[1,1152,6144]{2,1,0:T(8,128)(2,1)}, u32[]{:S(2)}) %copy-start) | copy-done | bytes 14155800
  101.6 5.2 %copy-done.1 = bf16[1,1152,6144]{2,1,0:T(8,128)(2,1)S(1)} copy-done((bf16[1,1152,6144]{2,1,0:T(8,128)(2,1)S(1)}, bf16[1,1152,6144]{2,1,0:T(8,128)(2,1)}, u32[]{:S(2)}) %copy-start.1) | copy-done | bytes 14155800
  106.8 2.9 %copy-done.29 = bf16[512,6144]{1,0:T(8,128)(2,1)S(1)} copy-done((bf16[512,6144]{1,0:T(8,128)(2,1)S(1)}, bf16[512,6144]{1,0:T(8,128)(2,1)}, u32[]{:S(2)}) %copy-start.29) | copy-done | bytes 6291480
  109.7 11.8 %backward_rows.1.refs_10_.refs_6_ = f32[512,1152]{1,0:T(8,128)S(1)} custom-call(bf16[512,6144]{1,0:T(8,128)(2,1)S(1)} %copy-done.29, bf16[1152,6144]{1,0:T(8,128)(2,1)S(1)} %bitcast.214, bf16[128,768]{1,0:T(8,128)(2,1)} %collective-permute-done.13.refs_0_, f32[512,1]{1,0:T(8,128)S(1)} %get-tuple-element.48.refs_1_.refs_9_), custom_call_target="tpu_custom_call" | custom-call | flops 7247757312 | bytes 14155776 | tf_op jit(solution)/shard_map/backward_rows/pallas_call | solution.py:201
  122.4 5.0 %before_rows.6 = (f32[512,1152]{1,0:T(8,128)S(1)}, f32[512,1]{1,0:T(8,128)S(1)}) custom-call(bf16[1152,6144]{1,0:T(8,128)(2,1)S(1)} %bitcast.205, f32[8,768]{1,0:T(8,128)S(1)} %reshape.364.gain_ref, bf16[128,768]{1,0:T(8,128)(2,1)S(1)} %copy-done.10, bf16[128,768]{1,0:T(8,128)(2,1)S(1)} %collective-permute-done.29.refs_1_, bf16[128,768]{1,0:T(8,128)(2,1)S(1)} %copy-done.16, ...), custom_call_target="tpu_custom_call" | custom-call | flops 1811939328 | bytes 3538944 | tf_op jit(solution)/shard_map/before_rows/pallas_call | solution.py:276
  128.0 4.3 %before_rows.7 = (f32[512,1152]{1,0:T(8,128)S(1)}, f32[512,1]{1,0:T(8,128)S(1)}) custom-call(bf16[1152,6144]{1,0:T(8,128)(2,1)S(1)} %bitcast.206, f32[8,768]{1,0:T(8,128)S(1)} %reshape.364.gain_ref, bf16[128,768]{1,0:T(8,128)(2,1)S(1)} %copy-done.8, bf16[128,768]{1,0:T(8,128)(2,1)} %collective-permute-done.23.refs_1_, ...), custom_call_target="tpu_custom_call" | custom-call | flops 1811939328 | bytes 3538944 | tf_op jit(solution)/shard_map/before_rows/pallas_call | solution.py:276
  132.3 4.1 %before_rows.8 = (f32[512,1152]{1,0:T(8,128)S(1)}, f32[512,1]{1,0:T(8,128)S(1)}) custom-call(bf16[1152,6144]{1,0:T(8,128)(2,1)S(1)} %bitcast.207, f32[8,768]{1,0:T(8,128)S(1)} %reshape.364.gain_ref, bf16[128,768]{1,0:T(8,128)(2,1)} %get-tuple-element.45.refs_4_.refs_0_, bf16[128,768]{1,0:T(8,128)(2,1)} %collective-permute-done.17.refs_1_, ...), custom_call_target="tpu_custom_call" | custom-call | flops 1811939328 | bytes 3538944 | tf_op jit(solution)/shard_map/before_rows/pallas_call | solution.py:276
  136.5 3.4 %before_rows.9 = (bf16[512,1152]{1,0:T(8,128)(2,1)S(1)}, bf16[512,1152]{1,0:T(8,128)(2,1)S(1)}) custom-call(bf16[1152,6144]{1,0:T(8,128)(2,1)S(1)} %bitcast.208, f32[8,768]{1,0:T(8,128)S(1)} %reshape.364.gain_ref, bf16[128,768]{1,0:T(8,128)(2,1)} %collective-permute-done.13.refs_0_, bf16[128,768]{1,0:T(8,128)(2,1)} %collective-permute-done.14.refs_1_, ...), custom_call_target="tpu_custom_call" | custom-call | flops 905969664 | bytes 1769472 | tf_op jit(solution)/shard_map/before_rows/pallas_call | solution.py:276
  166.4 5.0 %collective-permute-done.46.refs_1_ = bf16[2,128,768]{2,1,0:T(8,128)(2,1)S(1)} collective-permute-done((bf16[2,128,768]{2,1,0:T(8,128)(2,1)S(1)}, bf16[2,128,768]{2,1,0:T(8,128)(2,1)S(1)}, u32[]{:S(2)}, u32[]{:S(2)}) %collective-permute-start.46) | collective-permute-done | bytes 393248 | tf_op jit(solution)/shard_map/ppermute | solution.py:88
  183.2 7.7 %collective-permute-done.66 = bf16[256,768]{1,0:T(8,128)(2,1)S(1)} collective-permute-done((bf16[256,768]{1,0:T(8,128)(2,1)S(1)}, bf16[256,768]{1,0:T(8,128)(2,1)S(1)}, u32[]{:S(2)}, u32[]{:S(2)}) %collective-permute-start.66) | collective-permute-done | bytes 393248 | tf_op jit(solution)/shard_map/ppermute | solution.py:81
  198.0 8.2 %collective-permute-done.58 = bf16[128,768]{1,0:T(8,128)(2,1)S(1)} collective-permute-done((bf16[128,768]{1,0:T(8,128)(2,1)S(1)}, bf16[128,768]{1,0:T(8,128)(2,1)S(1)}, u32[]{:S(2)}, u32[]{:S(2)}) %collective-permute-start.58) | collective-permute-done | bytes 196640 | tf_op jit(solution)/shard_map/ppermute | solution.py:84
  217.7 6.1 %collective-permute-done.60 = f32[5,128]{1,0:T(8,128)S(1)} collective-permute-done((f32[5,128]{1,0:T(8,128)S(1)}, f32[5,128]{1,0:T(8,128)S(1)}, u32[]{:S(2)}, u32[]{:S(2)}) %collective-permute-start.60) | collective-permute-done | bytes 2592 | tf_op jit(solution)/shard_map/ppermute | solution.py:95
  223.8 3.6 %collective-permute-done.61 = f32[5,128]{1,0:T(8,128)S(1)} collective-permute-done((f32[5,128]{1,0:T(8,128)S(1)}, f32[5,128]{1,0:T(8,128)S(1)}, u32[]{:S(2)}, u32[]{:S(2)}) %collective-permute-start.61) | collective-permute-done | bytes 2592 | tf_op jit(solution)/shard_map/ppermute | solution.py:95
  231.9 3.1 %collective-permute-done.72 = bf16[128,768]{1,0:T(8,128)(2,1)S(1)} collective-permute-done((bf16[128,768]{1,0:T(8,128)(2,1)S(1)}, bf16[128,768]{1,0:T(8,128)(2,1)S(1)}, u32[]{:S(2)}, u32[]{:S(2)}) %collective-permute-start.72) | collective-permute-done | bytes 196640 | tf_op jit(solution)/shard_map/ppermute | solution.py:88
  242.1 4.5 %all-to-all-start.1 = ((bf16[8,32,768]{2,1,0:T(8,128)(2,1)}), bf16[8,32,768]{2,1,0:T(8,128)(2,1)S(1)}, u32[]{:S(2)}, u32[]{:S(2)}) async-start(bf16[8,32,768]{2,1,0:T(8,128)(2,1)} %pad_maximum_fusion.3), calls=%async_computation.1 | async-start | bytes 786432 | tf_op jit(solution)/shard_map/all_to_all | solution.py:500
  246.8 5.4 %collective-permute-done.74 = f32[8,96,96]{2,1,0:T(8,128)S(1)} collective-permute-done((f32[8,96,96]{2,1,0:T(8,128)S(1)}, f32[8,96,96]{2,1,0:T(8,128)S(1)}, u32[]{:S(2)}, u32[]{:S(2)}) %collective-permute-start.74) | collective-permute-done | bytes 294944 | tf_op jit(solution)/shard_map/ppermute | solution.py:507
  255.2 3.4 %all-to-all-done.1 = bf16[8,32,768]{2,1,0:T(8,128)(2,1)S(1)} async-done(((bf16[8,32,768]{2,1,0:T(8,128)(2,1)}), bf16[8,32,768]{2,1,0:T(8,128)(2,1)S(1)}, u32[]{:S(2)}, u32[]{:S(2)}) %all-to-all-start.1) | async-done | bytes 393248 | tf_op jit(solution)/shard_map/all_to_all | solution.py:500
  (353 shorter events, 133.7 us)
Async XLA Ops:
  7.2 94.4 %all-gather.2.cloned.1.call-start = ((), (), s32[]{:S(2)}) async-start(), calls=%async_computation.2 | async-start | bytes 6488064 | tf_op jit(solution)/shard_map/all_gather | solution.py:368
  23.6 20.0 %all-to-all-start = ((bf16[8,32,768]{2,1,0:T(8,128)(2,1)}), bf16[8,32,768]{2,1,0:T(8,128)(2,1)S(1)}, u32[]{:S(2)}, u32[]{:S(2)}) async-start(bf16[8,32,768]{2,1,0:T(8,128)(2,1)} %turn.1), calls=%async_computation | async-start | bytes 786432 | tf_op jit(solution)/shard_map/all_to_all | solution.py:384
  62.0 14.9 %collective-permute-start.32 = (bf16[128,768]{1,0:T(8,128)(2,1)}, bf16[128,768]{1,0:T(8,128)(2,1)S(1)}, u32[]{:S(2)}, u32[]{:S(2)}) collective-permute-start(bf16[128,768]{1,0:T(8,128)(2,1)} %get-tuple-element.42.refs_4_), channel_id=1, source_target_pairs={{0,2},{1,3},{2,0},{3,1},{4,6},{5,7},{6,4},{7,5},{8,10},{9,11},{10,... | collective-permute-start | bytes 589832 | tf_op jit(solution)/shard_map/ppermute | solution.py:88
  81.2 15.9 %collective-permute-start.26 = (bf16[128,768]{1,0:T(8,128)(2,1)}, bf16[128,768]{1,0:T(8,128)(2,1)}, u32[]{:S(2)}, u32[]{:S(2)}) collective-permute-start(bf16[128,768]{1,0:T(8,128)(2,1)} %get-tuple-element.44.refs_4_), channel_id=1, source_target_pairs={{0,2},{1,3},{2,0},{3,1},{4,6},{5,7},{6,4},{7,5},{8,10},{9,11},{10,... | collective-permute-start | bytes 589832 | tf_op jit(solution)/shard_map/ppermute | solution.py:88
  82.6 16.7 %collective-permute-start.24 = (bf16[128,768]{1,0:T(8,128)(2,1)}, bf16[128,768]{1,0:T(8,128)(2,1)}, u32[]{:S(2)}, u32[]{:S(2)}) collective-permute-start(bf16[128,768]{1,0:T(8,128)(2,1)} %get-tuple-element.43.refs_0_), channel_id=1, source_target_pairs={{0,1},{1,0},{2,3},{3,2},{4,5},{5,4},{6,7},{7,6},{8,9},{9,8},{10,11... | collective-permute-start | bytes 589832 | tf_op jit(solution)/shard_map/ppermute | solution.py:88
  83.3 16.2 %collective-permute-start.27 = (bf16[128,768]{1,0:T(8,128)(2,1)}, bf16[128,768]{1,0:T(8,128)(2,1)}, u32[]{:S(2)}, u32[]{:S(2)}) collective-permute-start(bf16[128,768]{1,0:T(8,128)(2,1)} %get-tuple-element.44.refs_4_), channel_id=1, source_target_pairs={{0,1},{1,0},{2,3},{3,2},{4,5},{5,4},{6,7},{7,6},{8,9},{9,8},{10,11... | collective-permute-start | bytes 589832 | tf_op jit(solution)/shard_map/ppermute | solution.py:88
  84.5 15.4 %collective-permute-start.13 = (bf16[128,768]{1,0:T(8,128)(2,1)}, bf16[128,768]{1,0:T(8,128)(2,1)}, u32[]{:S(2)}, u32[]{:S(2)}) collective-permute-start(bf16[128,768]{1,0:T(8,128)(2,1)} %get-tuple-element.45.refs_4_.refs_0_), channel_id=1, source_target_pairs={{0,8},{8,16},{16,24},{24,28},{28,20},{20,12},{12,4},{4,0},{1,9},{9... | collective-permute-start | bytes 589832 | tf_op jit(solution)/shard_map/ppermute | solution.py:81
  97.1 24.7 %collective-permute-start.17 = (bf16[128,768]{1,0:T(8,128)(2,1)}, bf16[128,768]{1,0:T(8,128)(2,1)}, u32[]{:S(2)}, u32[]{:S(2)}) collective-permute-start(bf16[128,768]{1,0:T(8,128)(2,1)} %get-tuple-element.45.refs_4_.refs_0_), channel_id=1, source_target_pairs={{0,2},{1,3},{2,0},{3,1},{4,6},{5,7},{6,4},{7,5},{8,10},{9,11},{10,... | collective-permute-start | bytes 589832 | tf_op jit(solution)/shard_map/ppermute | solution.py:88
  99.2 28.2 %collective-permute-start.18 = (bf16[128,768]{1,0:T(8,128)(2,1)}, bf16[128,768]{1,0:T(8,128)(2,1)}, u32[]{:S(2)}, u32[]{:S(2)}) collective-permute-start(bf16[128,768]{1,0:T(8,128)(2,1)} %get-tuple-element.45.refs_4_.refs_0_), channel_id=1, source_target_pairs={{0,1},{1,0},{2,3},{3,2},{4,5},{5,4},{6,7},{7,6},{8,9},{9,8},{10,11... | collective-permute-start | bytes 589832 | tf_op jit(solution)/shard_map/ppermute | solution.py:88
  99.5 22.7 %collective-permute-start.20 = (bf16[128,768]{1,0:T(8,128)(2,1)S(1)}, bf16[128,768]{1,0:T(8,128)(2,1)}, u32[]{:S(2)}, u32[]{:S(2)}) collective-permute-start(bf16[128,768]{1,0:T(8,128)(2,1)S(1)} %copy-done.4), channel_id=1, source_target_pairs={{0,2},{1,3},{2,0},{3,1},{4,6},{5,7},{6,4},{7,5},{8,10},{9,11},{10,... | collective-permute-start | bytes 589832 | tf_op jit(solution)/shard_map/ppermute | solution.py:88
  99.9 21.7 %collective-permute-start.28 = (bf16[128,768]{1,0:T(8,128)(2,1)}, bf16[128,768]{1,0:T(8,128)(2,1)}, u32[]{:S(2)}, u32[]{:S(2)}) collective-permute-start(bf16[128,768]{1,0:T(8,128)(2,1)} %collective-permute-done.26.refs_5_), channel_id=1, source_target_pairs={{0,1},{1,0},{2,3},{3,2},{4,5},{5,4},{6,7},{7,6},{8,9},{9,8},{10,11... | collective-permute-start | bytes 589832 | tf_op jit(solution)/shard_map/ppermute | solution.py:88
  99.9 28.0 %collective-permute-start.14 = (bf16[128,768]{1,0:T(8,128)(2,1)}, bf16[128,768]{1,0:T(8,128)(2,1)}, u32[]{:S(2)}, u32[]{:S(2)}) collective-permute-start(bf16[128,768]{1,0:T(8,128)(2,1)} %collective-permute-done.13.refs_0_), channel_id=1, source_target_pairs={{0,2},{1,3},{2,0},{3,1},{4,6},{5,7},{6,4},{7,5},{8,10},{9,11},{10,... | collective-permute-start | bytes 589832 | tf_op jit(solution)/shard_map/ppermute | solution.py:88
  146.5 25.0 %collective-permute-start.44 = (bf16[128,768]{1,0:T(8,128)(2,1)S(1)}, bf16[128,768]{1,0:T(8,128)(2,1)S(1)}, u32[]{:S(2)}, u32[]{:S(2)}) collective-permute-start(bf16[128,768]{1,0:T(8,128)(2,1)S(1)} %get-tuple-element.117), channel_id=1, source_target_pairs={{0,8},{8,16},{16,24},{24,28},{28,20},{20,12},{12,4},{4,0},{1,9},{9... | collective-permute-start | bytes 589832 | tf_op jit(solution)/shard_map/ppermute | solution.py:81
  147.7 24.3 %collective-permute-start.45 = (bf16[128,768]{1,0:T(8,128)(2,1)S(1)}, bf16[128,768]{1,0:T(8,128)(2,1)S(1)}, u32[]{:S(2)}, u32[]{:S(2)}) collective-permute-start(bf16[128,768]{1,0:T(8,128)(2,1)S(1)} %get-tuple-element.118), channel_id=1, source_target_pairs={{8,0},{16,8},{24,16},{28,24},{20,28},{12,20},{4,12},{0,4},{9,1},{1... | collective-permute-start | bytes 589832 | tf_op jit(solution)/shard_map/ppermute | solution.py:84
  163.6 18.0 %collective-permute-start.63 = (bf16[2,256,768]{2,1,0:T(8,128)(2,1)S(1)}, bf16[2,256,768]{2,1,0:T(8,128)(2,1)S(1)}, u32[]{:S(2)}, u32[]{:S(2)}) collective-permute-start(bf16[2,256,768]{2,1,0:T(8,128)(2,1)S(1)} %get-tuple-element.62.refs_0_), channel_id=1, source_target_pairs={{0,1},{1,0},{2,3},{3,2},{4,5},{5,4},{6,7},{7,6},{8,9},{9,8},{10,11... | collective-permute-start | bytes 2359304 | tf_op jit(solution)/shard_map/ppermute | solution.py:88
  165.1 15.5 %collective-permute-start.51 = (bf16[2,128,768]{2,1,0:T(8,128)(2,1)S(1)}, bf16[2,128,768]{2,1,0:T(8,128)(2,1)S(1)}, u32[]{:S(2)}, u32[]{:S(2)}) collective-permute-start(bf16[2,128,768]{2,1,0:T(8,128)(2,1)S(1)} %pad_maximum_fusion.2), channel_id=1, source_target_pairs={{0,2},{1,3},{2,0},{3,1},{4,6},{5,7},{6,4},{7,5},{8,10},{9,11},{10,... | collective-permute-start | bytes 1179656 | tf_op jit(solution)/shard_map/ppermute | solution.py:88
  178.9 30.9 %collective-permute-start.65 = (bf16[2,256,768]{2,1,0:T(8,128)(2,1)S(1)}, bf16[2,256,768]{2,1,0:T(8,128)(2,1)S(1)}, u32[]{:S(2)}, u32[]{:S(2)}) collective-permute-start(bf16[2,256,768]{2,1,0:T(8,128)(2,1)S(1)} %get-tuple-element.66.refs_0_), channel_id=1, source_target_pairs={{0,1},{1,0},{2,3},{3,2},{4,5},{5,4},{6,7},{7,6},{8,9},{9,8},{10,11... | collective-permute-start | bytes 2359304 | tf_op jit(solution)/shard_map/ppermute | solution.py:88
  190.9 15.3 %collective-permute-start.50 = (bf16[2,128,768]{2,1,0:T(8,128)(2,1)S(1)}, bf16[2,128,768]{2,1,0:T(8,128)(2,1)S(1)}, u32[]{:S(2)}, u32[]{:S(2)}) collective-permute-start(bf16[2,128,768]{2,1,0:T(8,128)(2,1)S(1)} %pad_maximum_fusion.1), channel_id=1, source_target_pairs={{0,2},{1,3},{2,0},{3,1},{4,6},{5,7},{6,4},{7,5},{8,10},{9,11},{10,... | collective-permute-start | bytes 1179656 | tf_op jit(solution)/shard_map/ppermute | solution.py:88
  191.9 15.7 %collective-permute-start.67 = (bf16[256,768]{1,0:T(8,128)(2,1)S(1)}, bf16[256,768]{1,0:T(8,128)(2,1)S(1)}, u32[]{:S(2)}, u32[]{:S(2)}) collective-permute-start(bf16[256,768]{1,0:T(8,128)(2,1)S(1)} %get-tuple-element.101), channel_id=1, source_target_pairs={{0,8},{8,16},{16,24},{24,28},{28,20},{20,12},{12,4},{4,0},{1,9},{9... | collective-permute-start | bytes 1179656 | tf_op jit(solution)/shard_map/ppermute | solution.py:81
  193.8 15.2 %collective-permute-start.70 = (bf16[256,768]{1,0:T(8,128)(2,1)S(1)}, bf16[256,768]{1,0:T(8,128)(2,1)S(1)}, u32[]{:S(2)}, u32[]{:S(2)}) collective-permute-start(bf16[256,768]{1,0:T(8,128)(2,1)S(1)} %get-tuple-element.102), channel_id=1, source_target_pairs={{8,0},{16,8},{24,16},{28,24},{20,28},{12,20},{4,12},{0,4},{9,1},{1... | collective-permute-start | bytes 1179656 | tf_op jit(solution)/shard_map/ppermute | solution.py:84
  206.2 22.7 %collective-permute-start.64 = (bf16[1,256,768]{2,1,0:T(8,128)(2,1)S(1)}, bf16[1,256,768]{2,1,0:T(8,128)(2,1)S(1)}, u32[]{:S(2)}, u32[]{:S(2)}) collective-permute-start(bf16[1,256,768]{2,1,0:T(8,128)(2,1)S(1)} %get-tuple-element.73), channel_id=1, source_target_pairs={{0,1},{1,0},{2,3},{3,2},{4,5},{5,4},{6,7},{7,6},{8,9},{9,8},{10,11... | collective-permute-start | bytes 1179656 | tf_op jit(solution)/shard_map/ppermute | solution.py:88
  211.0 18.0 %collective-permute-start.68 = (bf16[256,768]{1,0:T(8,128)(2,1)}, bf16[256,768]{1,0:T(8,128)(2,1)S(1)}, u32[]{:S(2)}, u32[]{:S(2)}) collective-permute-start(bf16[256,768]{1,0:T(8,128)(2,1)} %get-tuple-element.99), channel_id=1, source_target_pairs={{0,8},{8,16},{16,24},{24,28},{28,20},{20,12},{12,4},{4,0},{1,9},{9... | collective-permute-start | bytes 1179656 | tf_op jit(solution)/shard_map/ppermute | solution.py:81
  213.5 15.4 %collective-permute-start.71 = (bf16[256,768]{1,0:T(8,128)(2,1)}, bf16[256,768]{1,0:T(8,128)(2,1)S(1)}, u32[]{:S(2)}, u32[]{:S(2)}) collective-permute-start(bf16[256,768]{1,0:T(8,128)(2,1)} %get-tuple-element.100), channel_id=1, source_target_pairs={{8,0},{16,8},{24,16},{28,24},{20,28},{12,20},{4,12},{0,4},{9,1},{1... | collective-permute-start | bytes 1179656 | tf_op jit(solution)/shard_map/ppermute | solution.py:84
  242.1 16.5 %all-to-all-start.1 = ((bf16[8,32,768]{2,1,0:T(8,128)(2,1)}), bf16[8,32,768]{2,1,0:T(8,128)(2,1)S(1)}, u32[]{:S(2)}, u32[]{:S(2)}) async-start(bf16[8,32,768]{2,1,0:T(8,128)(2,1)} %pad_maximum_fusion.3), calls=%async_computation.1 | async-start | bytes 786432 | tf_op jit(solution)/shard_map/all_to_all | solution.py:500
  (112 other events, 865.3 us)
Sparse Core Ops, SparseCore 0:
  11.0 81.2 all-gather.1
